TPU v7x, 512 devices: a whole 4x4x16 slice. The times are simulated.
512 devices in a mesh: ens: 16 (over x, y), tile: 32 (over z, core).
Axes of the slice: x: 4, y: 4, z: 16, core: 2. Of those that a mesh axis runs over, the one named last changes fastest.
Arguments:
- air_latent_array: bfloat16 [16, 32, 64, 384], P('ens', 'tile'), may hold values from -6 to 6
- air_exchange_projection: bfloat16 [384, 128], replicated, may hold values from -0.3125 to 0.3125
- marine_latent_array: bfloat16 [16, 128, 256, 256], P('ens', None, 'tile'), may hold values from -6 to 6
- driver_projection_matrix: bfloat16 [128, 256], replicated, may hold values from -0.5 to 0.5
- spatial_kernel_taps: float32 [9, 256], replicated, may hold values from -1.5 to 1.5
- layernorm_multiplier: float32 [256], replicated, may hold values from 0.25 to 1.75
- pointwise_widen_matrix: bfloat16 [256, 1024], replicated, may hold values from -0.375 to 0.375
- pointwise_shrink_matrix: bfloat16 [1024, 256], replicated, may hold values from -0.1875 to 0.1875
- thermal_projection_matrix: bfloat16 [256, 128], replicated, may hold values from -0.375 to 0.375
- intersecting_air_sites: int32 [4, 128, 256], P(None, None, 'tile'), may hold values from 0 to 63, as said below
- margin_multiplier: int32 [4, 128, 256], P(None, None, 'tile'), may hold values from 1 to 8
- terrain_water_indicator: int32 [128, 256], P(None, 'tile'), may hold values from 0 to 1, as said below
- marine_successor_adjoint: bfloat16 [16, 128, 256, 256], P('ens', None, 'tile'), may hold values from -6 to 6
Outputs:
- marine_successor_latent: bfloat16 [16, 128, 256, 256], P('ens', None, 'tile')
- sst_atm: bfloat16 [16, 32, 64, 128], P('ens', 'tile')
- marine_latent_adjoint: bfloat16 [16, 128, 256, 256], P('ens', None, 'tile')
- grad_force: bfloat16 [128, 256], replicated
- grad_conv: bfloat16 [9, 256], replicated
- grad_gain: bfloat16 [256], replicated
- grad_up: bfloat16 [256, 1024], replicated
- grad_down: bfloat16 [1024, 256], replicated
Inputs may be any that keep to these rules, and one draw needn't show every extreme that they name: `intersecting_air_sites`: the index of an atmosphere cell that lies over the ocean cell's own tile: row * 2 + column, with the row among all 32 rows and the column among the 2 atmosphere columns over that tile. `terrain_water_indicator`: 1 marks a sea cell, 0 a land cell.
All inputs are finite; a program needn't handle non-finite values.
Results may differ from a plain program's by a relative error of at most 0.0082.
Values may be sent and summed in bfloat16 or wider, within the bound.
No kernel may reach another device: no remote copies, remote signals or barrier semaphores. Data moves between devices by JAX's collectives and lax.ppermute only.
A program may use at most 64 MiB of HBM per device.

v0:
```python
import math

import jax
import jax.numpy as jnp
from jax import lax
from jax.sharding import Mesh
from jax.sharding import PartitionSpec as P

SUBDIVISION = 4
KS = 3
TILE = ("tile_0", "tile_1")
ENS = ("ens_0", "ens_1")


def extended(cells, sides, width):
    for axis, dim in sides:
        count = lax.axis_size(axis)
        head = lax.slice_in_dim(cells, 0, width, axis=dim)
        tail = lax.slice_in_dim(cells, cells.shape[dim] - width, cells.shape[dim], axis=dim)
        cells = jnp.concatenate(
            [
                lax.ppermute(tail, axis, [(i, (i + 1) % count) for i in range(count)]),
                cells,
                lax.ppermute(head, axis, [((i + 1) % count, i) for i in range(count)]),
            ],
            axis=dim,
        )
    return cells


def split_up(value, dim, peers):
    before, after = (value.shape[:dim], value.shape[dim + 1 :])
    return jnp.moveaxis(value.reshape(*before, peers, -1, *after), dim, 0)


def summed_on_arrival(value, axis, dim):
    peers = lax.axis_size(axis)
    pieces = lax.all_to_all(split_up(value, dim, peers), axis, 0, 0, tiled=True)
    return jnp.sum(pieces, axis=0)


def summed_rows(value, axes, dim):
    far, near = axes
    own = summed_on_arrival(split_up(value, dim, lax.axis_size(far)), near, dim + 1)
    return jnp.sum(lax.all_to_all(own, far, 0, 0, tiled=True), axis=0)


def rows_for(lines, peers):
    spare = -lines.shape[0] % peers
    if not spare:
        return lines
    return jnp.concatenate([lines, jnp.zeros((spare, *lines.shape[1:]), lines.dtype)])


def copy_for_each(value, axis):
    peers = lax.axis_size(axis)
    return lax.all_to_all(
        jnp.broadcast_to(value[None], (peers, *value.shape)), axis, 0, 0, tiled=True
    )


def laid_out(pieces, dim):
    shape = list(pieces.shape[1:])
    shape[dim] *= pieces.shape[0]
    return jnp.moveaxis(pieces, 0, dim).reshape(shape)


def whole_of(value, axes, dim):
    far, near = axes
    leading = copy_for_each(value, far)
    pieces = jnp.swapaxes(copy_for_each(leading, near), 0, 1)
    return laid_out(pieces.reshape(-1, *value.shape), dim)


def nested_sum(value, axes):
    own = summed_rows(rows_for(value, lax.axis_size(axes[0]) * lax.axis_size(axes[1])), axes, 0)
    whole = whole_of(own, axes, 0)
    return whole[: len(value)].reshape(value.shape)


def in_one(arrays, axis):
    vector, at, gathered = (jnp.concatenate([a.reshape(-1) for a in arrays]), 0, [])
    total = nested_sum(vector, axis)
    for a in arrays:
        gathered.append(total[at : at + a.size].reshape(a.shape))
        at += a.size
    return tuple(gathered)


def layer_norm(values, gain):
    centred = values - jnp.mean(values, axis=-1, keepdims=True)
    spread = jnp.mean(centred * centred, axis=-1, keepdims=True)
    return centred * lax.rsqrt(spread + 1e-06) * gain


def regrid(flat_fluxes, cell_ids, margin):
    picked = jnp.take(flat_fluxes, cell_ids, axis=0).astype(jnp.float32)
    factor = margin.astype(jnp.float32)
    weighted = jnp.sum(factor[..., None] * picked, axis=0)
    return (weighted / jnp.sum(factor, axis=0)[..., None]).astype(jnp.bfloat16)


def marine_update_kernel(
    marine_present_latent,
    marine_driver_input,
    latent_adjoint,
    water_indicator_real,
    driver_projection_matrix,
    spatial_kernel_taps,
    layernorm_multiplier,
    pointwise_widen_matrix,
    pointwise_shrink_matrix,
    thermal_projection_matrix,
    haloed_latent,
    haloed_derivative,
):
    horizontal_sum_result, vertical_sum_result, feature_dimension = marine_present_latent.shape
    reach = KS // 2
    forcing_flat = marine_driver_input.reshape(-1, marine_driver_input.shape[-1])
    pushed = jnp.dot(
        forcing_flat, driver_projection_matrix, preferred_element_type=jnp.float32
    ).reshape(horizontal_sum_result, vertical_sum_result, feature_dimension)
    mixed = (marine_present_latent.astype(jnp.float32) + pushed).astype(jnp.bfloat16)
    padded = jnp.pad(haloed_latent(mixed), ((reach, reach), (0, 0), (0, 0))).astype(jnp.float32)
    conv_out = jnp.zeros(
        (horizontal_sum_result, vertical_sum_result, feature_dimension), jnp.float32
    )
    for row_off in range(KS):
        for col_off in range(KS):
            conv_out = (
                conv_out
                + spatial_kernel_taps[row_off * KS + col_off]
                * padded[
                    row_off : row_off + horizontal_sum_result,
                    col_off : col_off + vertical_sum_result,
                ]
            )
    normed_f, pull_norm = jax.vjp(
        layer_norm, conv_out.reshape(-1, feature_dimension), layernorm_multiplier
    )
    normed = normed_f.astype(jnp.bfloat16)
    hidden_pre = jnp.dot(normed, pointwise_widen_matrix, preferred_element_type=jnp.float32)
    hidden_f, pull_gelu = jax.vjp(jax.nn.gelu, hidden_pre)
    hidden = hidden_f.astype(jnp.bfloat16)
    mlp_out = jnp.dot(hidden, pointwise_shrink_matrix, preferred_element_type=jnp.float32)
    sea_column = water_indicator_real.reshape(-1, 1)
    marine_successor_latent = (
        sea_column * (mixed.reshape(-1, feature_dimension).astype(jnp.float32) + mlp_out)
    ).astype(jnp.bfloat16)
    thermal_highres_field = jnp.dot(
        marine_successor_latent, thermal_projection_matrix, preferred_element_type=jnp.float32
    )
    thermal_highres_field = thermal_highres_field.reshape(
        horizontal_sum_result // SUBDIVISION,
        SUBDIVISION,
        vertical_sum_result // SUBDIVISION,
        SUBDIVISION,
        thermal_highres_field.shape[-1],
    )
    marine_site_number = jnp.sum(
        water_indicator_real.reshape(
            horizontal_sum_result // SUBDIVISION,
            SUBDIVISION,
            vertical_sum_result // SUBDIVISION,
            SUBDIVISION,
        ),
        axis=(1, 3),
    )
    thermal_lowres_field = (
        jnp.sum(thermal_highres_field, axis=(1, 3))
        / jnp.maximum(marine_site_number, 1.0)[..., None]
    ).astype(jnp.bfloat16)
    masked_cot = (
        sea_column * latent_adjoint.reshape(-1, feature_dimension).astype(jnp.float32)
    ).astype(jnp.bfloat16)
    grad_down = jnp.dot(hidden.T, masked_cot, preferred_element_type=jnp.float32)
    hidden_cot = jnp.dot(masked_cot, pointwise_shrink_matrix.T, preferred_element_type=jnp.float32)
    pre_cot = pull_gelu(hidden_cot)[0].astype(jnp.bfloat16)
    grad_up = jnp.dot(normed.T, pre_cot, preferred_element_type=jnp.float32)
    normed_cot = jnp.dot(pre_cot, pointwise_widen_matrix.T, preferred_element_type=jnp.float32)
    conv_cot, grad_gain = pull_norm(normed_cot)
    conv_cot = conv_cot.reshape(horizontal_sum_result, vertical_sum_result, feature_dimension)
    tap_grads = []
    for row_off in range(KS):
        for col_off in range(KS):
            tap_grads.append(
                jnp.sum(
                    conv_cot
                    * padded[
                        row_off : row_off + horizontal_sum_result,
                        col_off : col_off + vertical_sum_result,
                    ],
                    axis=(0, 1),
                )
            )
    grad_padded = jnp.pad(haloed_derivative(conv_cot), ((reach, reach), (0, 0), (0, 0)))
    back = masked_cot.astype(jnp.float32).reshape(
        horizontal_sum_result, vertical_sum_result, feature_dimension
    )
    for row_off in range(KS):
        for col_off in range(KS):
            row_from = KS - 1 - row_off
            col_from = KS - 1 - col_off
            back = (
                back
                + spatial_kernel_taps[row_off * KS + col_off]
                * grad_padded[
                    row_from : row_from + horizontal_sum_result,
                    col_from : col_from + vertical_sum_result,
                ]
            )
    marine_latent_adjoint = back.astype(jnp.bfloat16)
    grad_force = jnp.dot(
        forcing_flat.T,
        marine_latent_adjoint.reshape(-1, feature_dimension),
        preferred_element_type=jnp.float32,
    )
    derivative_sequence = (grad_force, jnp.stack(tap_grads), grad_gain, grad_up, grad_down)
    return (
        marine_successor_latent.reshape(
            horizontal_sum_result, vertical_sum_result, feature_dimension
        ),
        thermal_lowres_field,
        marine_latent_adjoint,
        derivative_sequence,
    )


def pad_state_cols(values):
    return extended(values, ((TILE, 1),), KS // 2)


def pad_grad_cols(values):
    return extended(values, ((TILE, 1),), KS // 2)


def body(
    air_latent_array,
    air_exchange_projection,
    marine_latent_array,
    driver_projection_matrix,
    spatial_kernel_taps,
    layernorm_multiplier,
    pointwise_widen_matrix,
    pointwise_shrink_matrix,
    thermal_projection_matrix,
    intersecting_air_sites,
    margin_multiplier,
    terrain_water_indicator,
    marine_successor_adjoint,
):
    band = air_latent_array[0]
    band_rows, band_cols, atmos_width = band.shape
    fluxes = jnp.dot(
        band.reshape(-1, atmos_width), air_exchange_projection, preferred_element_type=jnp.float32
    ).astype(jnp.bfloat16)
    fluxes = fluxes.reshape(band_rows, band_cols, fluxes.shape[-1])
    strip = lax.all_to_all(fluxes, TILE, split_axis=1, concat_axis=0, tiled=True)
    marine_driver_input = regrid(
        strip.reshape(-1, strip.shape[-1]), intersecting_air_sites, margin_multiplier
    )
    water_indicator_real = terrain_water_indicator.astype(jnp.float32)
    marine_successor_latent, thermal_lowres_field, marine_latent_adjoint, derivative_sequence = (
        marine_update_kernel(
            marine_latent_array[0],
            marine_driver_input,
            marine_successor_adjoint[0],
            water_indicator_real,
            driver_projection_matrix,
            spatial_kernel_taps,
            layernorm_multiplier,
            pointwise_widen_matrix,
            pointwise_shrink_matrix,
            thermal_projection_matrix,
            pad_state_cols,
            pad_grad_cols,
        )
    )
    thermal_strip_slice = lax.all_to_all(
        thermal_lowres_field, TILE, split_axis=0, concat_axis=1, tiled=True
    )
    cell_total = (
        lax.axis_size(ENS)
        * lax.axis_size(TILE)
        * marine_successor_latent.shape[0]
        * marine_successor_latent.shape[1]
    )
    grad_scale = 1.0 / math.sqrt(cell_total)
    grad_force, grad_conv, grad_gain, grad_up, grad_down = derivative_sequence
    accumulated_result = in_one(
        (grad_force, grad_conv, grad_gain, grad_up, grad_down),
        (("ens_0", "ens_1"), ("tile_0", "tile_1")),
    )
    scaled = [(values * grad_scale).astype(jnp.bfloat16) for values in accumulated_result]
    return (
        marine_successor_latent[None],
        thermal_strip_slice[None],
        marine_latent_adjoint[None],
        scaled[0],
        scaled[1],
        scaled[2],
        scaled[3],
        scaled[4],
    )


def solution(mesh):
    finer = Mesh(mesh.devices.reshape(4, 4, 16, 2), ("ens_0", "ens_1", "tile_0", "tile_1"))
    return jax.shard_map(
        body,
        mesh=finer,
        in_specs=(
            P(ENS, TILE, None, None),
            P(),
            P(ENS, None, TILE, None),
            P(),
            P(),
            P(),
            P(),
            P(),
            P(),
            P(None, None, TILE),
            P(None, None, TILE),
            P(None, TILE),
            P(ENS, None, TILE, None),
        ),
        out_specs=(
            P(ENS, None, TILE, None),
            P(ENS, TILE, None, None),
            P(ENS, None, TILE, None),
            P(),
            P(),
            P(),
            P(),
            P(),
        ),
        check_vma=False,
    )
```

profile of v0, /device:TPU:1, one launch (start us, length us, event | category | flops | bytes accessed | tf_op | source)
XLA Modules:
  0.0 384.2 jit_solution(17312837534611754737)
XLA Ops:
  2.4 16.8 %all-to-all-start = ((bf16[32,2,128]{2,1,0:T(2,128)(2,1)}), bf16[32,2,128]{2,1,0:T(2,128)(2,1)S(1)}, u32[]{:S(2)}, u32[]{:S(2)}) async-start(bf16[32,2,128]{2,1,0:T(2,128)(2,1)} %bitcast.99), calls=%async_computation | async-start | bytes 32768 | tf_op jit(solution)/shard_map/all_to_all | solution.py:258
  24.3 6.7 %all-to-all-done = bf16[32,2,128]{2,1,0:T(2,128)(2,1)S(1)} async-done(((bf16[32,2,128]{2,1,0:T(2,128)(2,1)}), bf16[32,2,128]{2,1,0:T(2,128)(2,1)S(1)}, u32[]{:S(2)}, u32[]{:S(2)}) %all-to-all-start) | async-done | bytes 16416 | tf_op jit(solution)/shard_map/all_to_all | solution.py:258
  30.9 12.1 %gather_fusion = bf16[4096,128]{1,0:T(8,128)(2,1)S(1)} fusion(bf16[64,128]{1,0:T(8,128)(2,1)S(1)} %bitcast.100, s32[4096]{0:T(1024)S(1)} %broadcast_clamp_fusion), kind=kCustom, calls=%fused_computation | custom fusion | bytes 2113536 | tf_op jit(solution)/shard_map/jit(_take)/gather | solution.py:97
  49.2 2.7 collective-permute-done.1
  57.2 4.2 %fusion.6 = bf16[1024,1024]{1,0:T(8,128)(2,1)S(1)} fusion(f32[1024,1024]{1,0:T(8,128)S(1)} %fusion.39, bf16[1024,256]{1,0:T(8,128)(2,1)S(1)} %copy-done.29, f32[1,128,8,256]{3,1,2,0:T(8,128)S(1)} %copy-done.8, f32[1024]{0:T(1024)S(1)} %mul.332), kind=kOutput, calls=%fused_computation.9 | convolution fusion | flops 558366720 | bytes 7868416 | tf_op jit(solution)/shard_map/dot_general | solution.py:177
  70.9 2.2 fusion.15
  77.0 2.4 constant_dynamic-update-slice_fusion.1
  79.4 2.3 constant_dynamic-update-slice_fusion
  81.7 3.4 reshape_reshape.6
  85.1 2.8 copy.150
  87.9 7.0 %all-to-all-start.2 = ((f32[32,16,1093]{2,1,0:T(8,128)}), f32[32,16,1093]{2,1,0:T(8,128)S(1)}, u32[]{:S(2)}, u32[]{:S(2)}) async-start(f32[32,16,1093]{2,1,0:T(8,128)} %copy.150), calls=%async_computation.2 | async-start | bytes 4718592 | tf_op jit(solution)/shard_map/all_to_all | solution.py:38
  95.8 5.3 %fusion.9 = bf16[1024,256]{1,0:T(8,128)(2,1)} fusion(bf16[1024,256]{1,0:T(8,128)(2,1)} %param.20, f32[128,8,256]{2,0,1:T(8,128)} %get-tuple-element.78, f32[1024]{0:T(1024)S(1)} %copy-done.26, f32[1024,1024]{1,0:T(8,128)} %copy-done.4), kind=kOutput, calls=%fused_computation.23 | convolution fusion | flops 547094528 | bytes 6295552 | tf_op jit(solution)/shard_map/dot_general | solution.py:145
  101.1 103.3 %all-to-all-done.2 = f32[32,16,1093]{2,1,0:T(8,128)S(1)} async-done(((f32[32,16,1093]{2,1,0:T(8,128)}), f32[32,16,1093]{2,1,0:T(8,128)S(1)}, u32[]{:S(2)}, u32[]{:S(2)}) %all-to-all-start.2) | async-done | bytes 2238496 | tf_op jit(solution)/shard_map/all_to_all | solution.py:38
  205.2 6.8 %all-to-all-start.3 = ((f32[16,1,1093]{2,1,0:T(1,128)}), f32[16,1,1093]{2,1,0:T(1,128)S(1)}, u32[]{:S(2)}, u32[]{:S(2)}) async-start(f32[16,1,1093]{2,1,0:T(1,128)} %all_to_all.33), calls=%async_computation.3 | async-start | bytes 147456 | tf_op jit(solution)/shard_map/all_to_all | solution.py:45
  213.5 5.0 %all-to-all-done.3 = f32[16,1,1093]{2,1,0:T(1,128)S(1)} async-done(((f32[16,1,1093]{2,1,0:T(1,128)}), f32[16,1,1093]{2,1,0:T(1,128)S(1)}, u32[]{:S(2)}, u32[]{:S(2)}) %all-to-all-start.3) | async-done | bytes 69984 | tf_op jit(solution)/shard_map/all_to_all | solution.py:45
  219.3 3.5 all-to-all-start.4
  224.2 5.1 %all-to-all-done.4 = f32[16,1,1093]{2,1,0:T(1,128)S(1)} async-done(((f32[16,1,1093]{2,1,0:T(1,128)}), f32[16,1,1093]{2,1,0:T(1,128)S(1)}, u32[]{:S(2)}, u32[]{:S(2)}) %all-to-all-start.4) | async-done | bytes 69984 | tf_op jit(solution)/shard_map/all_to_all | solution.py:57
  229.3 8.0 %all-to-all-start.1 = ((bf16[32,2,128]{2,1,0:T(2,128)(2,1)}), bf16[32,2,128]{2,1,0:T(2,128)(2,1)S(1)}, u32[]{:S(2)}, u32[]{:S(2)}) async-start(bf16[32,2,128]{2,1,0:T(2,128)(2,1)} %divide_convert_fusion.1), calls=%async_computation.1 | async-start | bytes 32768 | tf_op jit(solution)/shard_map/all_to_all | solution.py:279
  237.3 11.7 %all-to-all-done.1 = bf16[32,2,128]{2,1,0:T(2,128)(2,1)S(1)} async-done(((bf16[32,2,128]{2,1,0:T(2,128)(2,1)}), bf16[32,2,128]{2,1,0:T(2,128)(2,1)S(1)}, u32[]{:S(2)}, u32[]{:S(2)}) %all-to-all-start.1) | async-done | bytes 16416 | tf_op jit(solution)/shard_map/all_to_all | solution.py:279
  250.5 4.6 %all-to-all-start.5 = ((f32[32,16,1093]{2,1,0:T(8,128)}), f32[32,16,1093]{2,1,0:T(8,128)S(1)}, u32[]{:S(2)}, u32[]{:S(2)}) async-start(f32[32,16,1093]{2,1,0:T(8,128)} %broadcast_in_dim.53), calls=%async_computation.5 | async-start | bytes 4718592 | tf_op jit(solution)/shard_map/all_to_all | solution.py:57
  256.2 108.6 %all-to-all-done.5 = f32[32,16,1093]{2,1,0:T(8,128)S(1)} async-done(((f32[32,16,1093]{2,1,0:T(8,128)}), f32[32,16,1093]{2,1,0:T(8,128)S(1)}, u32[]{:S(2)}, u32[]{:S(2)}) %all-to-all-start.5) | async-done | bytes 2238496 | tf_op jit(solution)/shard_map/all_to_all | solution.py:57
  366.2 2.4 copy.151
  368.6 2.8 reshape_reshape.7
  371.4 3.5 slice.164
  (142 shorter events, 49.8 us)
Async XLA Ops:
  0.6 53.3 %copy-start = (bf16[256,1024]{1,0:T(8,128)(2,1)S(1)}, bf16[256,1024]{1,0:T(8,128)(2,1)}, u32[]{:S(2)}) copy-start(bf16[256,1024]{1,0:T(8,128)(2,1)} %param.19) | copy-start | bytes 1572868
  0.6 23.2 %copy-start.13 = (s32[4,128,8]{1,2,0:T(8,128)S(1)}, s32[4,128,8]{1,2,0:T(8,128)}, u32[]{:S(2)}) copy-start(s32[4,128,8]{1,2,0:T(8,128)} %param.23) | copy-start | bytes 49156
  2.4 28.5 %all-to-all-start = ((bf16[32,2,128]{2,1,0:T(2,128)(2,1)}), bf16[32,2,128]{2,1,0:T(2,128)(2,1)S(1)}, u32[]{:S(2)}, u32[]{:S(2)}) async-start(bf16[32,2,128]{2,1,0:T(2,128)(2,1)} %bitcast.99), calls=%async_computation | async-start | bytes 32768 | tf_op jit(solution)/shard_map/all_to_all | solution.py:258
  46.8 2.4 collective-permute-start
  47.9 4.0 %collective-permute-start.1 = (bf16[128,1,256]{2,0,1:T(8,128)(2,1)S(1)}, bf16[128,1,256]{2,0,1:T(8,128)(2,1)S(1)}, u32[]{:S(2)}, u32[]{:S(2)}) collective-permute-start(bf16[128,1,256]{2,0,1:T(8,128)(2,1)S(1)} %get-tuple-element.67), channel_id=1, source_target_pairs={{1,0},{2,1},{3,2},{4,3},{5,4},{6,5},{7,6},{8,7},{9,8},{10,9},{11,1... | collective-permute-start | bytes 196616 | tf_op jit(solution)/shard_map/ppermute | solution.py:24
  47.9 5.1 %copy-start.15 = (f32[1,256]{1,0:T(1,128)}, f32[1,256]{1,0:T(1,128)S(1)}, u32[]{:S(2)}) copy-start(f32[1,256]{1,0:T(1,128)S(1)} %get-tuple-element.68) | copy-start | bytes 3076
  47.9 5.1 %copy-start.16 = (f32[1,256]{1,0:T(1,128)}, f32[1,256]{1,0:T(1,128)S(1)}, u32[]{:S(2)}) copy-start(f32[1,256]{1,0:T(1,128)S(1)} %get-tuple-element.69) | copy-start | bytes 3076
  47.9 5.1 %copy-start.17 = (f32[1,256]{1,0:T(1,128)}, f32[1,256]{1,0:T(1,128)S(1)}, u32[]{:S(2)}) copy-start(f32[1,256]{1,0:T(1,128)S(1)} %get-tuple-element.70) | copy-start | bytes 3076
  47.9 5.1 %copy-start.18 = (f32[1,256]{1,0:T(1,128)}, f32[1,256]{1,0:T(1,128)S(1)}, u32[]{:S(2)}) copy-start(f32[1,256]{1,0:T(1,128)S(1)} %get-tuple-element.71) | copy-start | bytes 3076
  47.9 5.1 %copy-start.19 = (f32[1,256]{1,0:T(1,128)}, f32[1,256]{1,0:T(1,128)S(1)}, u32[]{:S(2)}) copy-start(f32[1,256]{1,0:T(1,128)S(1)} %get-tuple-element.72) | copy-start | bytes 3076
  47.9 5.1 %copy-start.20 = (f32[1,256]{1,0:T(1,128)}, f32[1,256]{1,0:T(1,128)S(1)}, u32[]{:S(2)}) copy-start(f32[1,256]{1,0:T(1,128)S(1)} %get-tuple-element.73) | copy-start | bytes 3076
  48.0 5.1 %copy-start.21 = (f32[1,256]{1,0:T(1,128)}, f32[1,256]{1,0:T(1,128)S(1)}, u32[]{:S(2)}) copy-start(f32[1,256]{1,0:T(1,128)S(1)} %get-tuple-element.74) | copy-start | bytes 3076
  48.0 5.1 %copy-start.22 = (f32[1,256]{1,0:T(1,128)}, f32[1,256]{1,0:T(1,128)S(1)}, u32[]{:S(2)}) copy-start(f32[1,256]{1,0:T(1,128)S(1)} %get-tuple-element.75) | copy-start | bytes 3076
  48.2 9.0 %copy-start.25 = (f32[1024]{0:T(1024)}, f32[1024]{0:T(1024)S(1)}, u32[]{:S(2)}) copy-start(f32[1024]{0:T(1024)S(1)} %mul.332) | copy-start | bytes 12292
  65.4 4.0 %collective-permute-start.2 = (f32[128,1,256]{2,0,1:T(8,128)S(1)}, f32[128,1,256]{2,0,1:T(8,128)S(1)}, u32[]{:S(2)}, u32[]{:S(2)}) collective-permute-start(f32[128,1,256]{2,0,1:T(8,128)S(1)} %get-tuple-element.64), channel_id=1, source_target_pairs={{0,1},{1,2},{2,3},{3,4},{4,5},{5,6},{6,7},{7,8},{8,9},{9,10},{10,1... | collective-permute-start | bytes 393224 | tf_op jit(solution)/shard_map/ppermute | solution.py:22
  65.4 4.7 %collective-permute-start.3 = (f32[128,1,256]{2,0,1:T(8,128)S(1)}, f32[128,1,256]{2,0,1:T(8,128)S(1)}, u32[]{:S(2)}, u32[]{:S(2)}) collective-permute-start(f32[128,1,256]{2,0,1:T(8,128)S(1)} %get-tuple-element.65), channel_id=1, source_target_pairs={{1,0},{2,1},{3,2},{4,3},{5,4},{6,5},{7,6},{8,7},{9,8},{10,9},{11,1... | collective-permute-start | bytes 393224 | tf_op jit(solution)/shard_map/ppermute | solution.py:24
  70.9 6.1 %copy-start.5 = (f32[32,8,8,128]{3,1,2,0:T(8,128)S(1)}, f32[32,8,8,128]{3,1,2,0:T(8,128)}, u32[]{:S(2)}) copy-start(f32[32,8,8,128]{3,1,2,0:T(8,128)} %copy.157) | copy-start | bytes 3145732
  87.9 7.9 %copy-start.26 = (f32[1024]{0:T(1024)S(1)}, f32[1024]{0:T(1024)}, u32[]{:S(2)}) copy-start(f32[1024]{0:T(1024)} %copy-done.25) | copy-start | bytes 12292
  87.9 116.5 %all-to-all-start.2 = ((f32[32,16,1093]{2,1,0:T(8,128)}), f32[32,16,1093]{2,1,0:T(8,128)S(1)}, u32[]{:S(2)}, u32[]{:S(2)}) async-start(f32[32,16,1093]{2,1,0:T(8,128)} %copy.150), calls=%async_computation.2 | async-start | bytes 4718592 | tf_op jit(solution)/shard_map/all_to_all | solution.py:38
  101.1 110.9 %copy-start.12 = (bf16[256,128]{1,0:T(8,128)(2,1)S(1)}, bf16[256,128]{1,0:T(8,128)(2,1)}, u32[]{:S(2)}) copy-start(bf16[256,128]{1,0:T(8,128)(2,1)} %param.21) | copy-start | bytes 196612
  205.2 13.3 %all-to-all-start.3 = ((f32[16,1,1093]{2,1,0:T(1,128)}), f32[16,1,1093]{2,1,0:T(1,128)S(1)}, u32[]{:S(2)}, u32[]{:S(2)}) async-start(f32[16,1,1093]{2,1,0:T(1,128)} %all_to_all.33), calls=%async_computation.3 | async-start | bytes 147456 | tf_op jit(solution)/shard_map/all_to_all | solution.py:45
  219.3 10.0 %all-to-all-start.4 = ((f32[16,1,1093]{2,1,0:T(1,128)}), f32[16,1,1093]{2,1,0:T(1,128)S(1)}, u32[]{:S(2)}, u32[]{:S(2)}) async-start(f32[16,1,1093]{2,1,0:T(1,128)} %broadcast_in_dim.51), calls=%async_computation.4 | async-start | bytes 147456 | tf_op jit(solution)/shard_map/all_to_all | solution.py:57
  229.3 19.7 %all-to-all-start.1 = ((bf16[32,2,128]{2,1,0:T(2,128)(2,1)}), bf16[32,2,128]{2,1,0:T(2,128)(2,1)S(1)}, u32[]{:S(2)}, u32[]{:S(2)}) async-start(bf16[32,2,128]{2,1,0:T(2,128)(2,1)} %divide_convert_fusion.1), calls=%async_computation.1 | async-start | bytes 32768 | tf_op jit(solution)/shard_map/all_to_all | solution.py:279
  250.5 114.3 %all-to-all-start.5 = ((f32[32,16,1093]{2,1,0:T(8,128)}), f32[32,16,1093]{2,1,0:T(8,128)S(1)}, u32[]{:S(2)}, u32[]{:S(2)}) async-start(f32[32,16,1093]{2,1,0:T(8,128)} %broadcast_in_dim.53), calls=%async_computation.5 | async-start | bytes 4718592 | tf_op jit(solution)/shard_map/all_to_all | solution.py:57
  (16 other events, 41.3 us)
where the time goes:
time: 386 us; the launch traced here: 384 us
  waiting for transfers between devices  245 us (63%)
  local copies, waits for them, and re-layouts  48.4 us (13%)
  starting transfers between devices  48.4 us (13%)
  other arithmetic  21.3 us (6%)
  matrix products  20 us (5%)
    all_to_all x2, waiting for transfers between devices, copy_for_each(): lax.all_to_all(jnp.broadcast_to(value[None], (peers, *value.shape)), axis...  114 us
    all_to_all x1, waiting for transfers between devices, summed_on_arrival(): pieces = lax.all_to_all(split_up(value, dim, peers), axis, 0, 0, tiled=True)  103 us
    all_to_all x1, starting transfers between devices, body(): lax.all_to_all(fluxes, TILE, split_axis=1, concat_axis=0, tiled=True)  16.8 us
    unnamed x73, local copies, waits for them, and re-layouts  12.8 us
    gather x1, local copies, waits for them, and re-layouts, regrid(): picked = jnp.take(flat_fluxes, cell_ids, axis=0).astype(jnp.float32)  12.1 us
    all_to_all x1, waiting for transfers between devices, body(): lax.all_to_all(thermal_lowres_field, TILE, split_axis=0, concat_axis=1, t...  11.7 us
    all_to_all x2, starting transfers between devices, copy_for_each(): lax.all_to_all(jnp.broadcast_to(value[None], (peers, *value.shape)), axis...  8.11 us
    all_to_all x1, starting transfers between devices, body(): lax.all_to_all(thermal_lowres_field, TILE, split_axis=0, concat_axis=1, t...  7.96 us
  transfers between devices with their start and end apart: 10, of which 9 were waited for; matrix products, arithmetic and copies ran while one was open for 5% of the time, Pallas kernels for 0%

commit v1 on v0

v1 whole, which is shorter than its diff:
```python
import functools
import math

import jax
import jax.numpy as jnp
from jax import lax
from jax.experimental import pallas as pl
from jax.experimental.pallas import tpu as pltpu
from jax.sharding import Mesh
from jax.sharding import PartitionSpec as P

F32 = jnp.float32
BF16 = jnp.bfloat16
ENS = ("ens_0", "ens_1")
TILE = ("tile_0", "tile_1")
Z, CORE = TILE

ROWS = 128
OWN = 8
CH = 256
HID = 1024
LINK = 128
MARGINS = 4
WIDE = OWN + 4
MID = OWN + 2
HALO = 3 * ROWS + 16
XY = 16
ZS = 16
BIG = 128
CHUNK = 152
PIECE = 16
GELU_A = math.sqrt(2.0 / math.pi)
GELU_B = GELU_A * 0.044715


def call(kernel, out_shape, scratch=(), limit=24, flops=0, moved=0, smem=(), far=()):
    def run(*args):
        args = [
            pltpu.with_memory_space_constraint(arg, pltpu.HBM) if i in far else arg
            for i, arg in enumerate(args)
        ]

        def space(i):
            if i in smem:
                return pltpu.SMEM
            return pltpu.HBM if i in far else pltpu.VMEM

        return pl.pallas_call(
            kernel,
            out_shape=out_shape,
            in_specs=[pl.BlockSpec(memory_space=space(i)) for i in range(len(args))],
            out_specs=jax.tree.map(lambda _: pl.BlockSpec(memory_space=pltpu.VMEM), out_shape),
            scratch_shapes=list(scratch),
            compiler_params=pltpu.CompilerParams(vmem_limit_bytes=limit * 2**20),
            cost_estimate=pl.CostEstimate(flops=flops, bytes_accessed=moved, transcendentals=0),
        )(*args)

    return run


def shape(*dims, dtype=BF16):
    return jax.ShapeDtypeStruct(dims, dtype)


def held(*dims, dtype=BF16):
    return pltpu.VMEM(dims, dtype)


def dot(a, b, contract=((1,), (0,))):
    return lax.dot_general(a, b, (contract, ((), ())), preferred_element_type=F32)


NT = ((1,), (1,))
TN = ((0,), (0,))


CELLS = ROWS * OWN


def put_rows(turned, value):
    flat = value.astype(F32).reshape(CELLS, CH)
    turned[pl.ds(0, CELLS), :] = flat[:, :128]
    turned[pl.ds(CELLS, CELLS), :] = flat[:, 128:]


def column(turned, c):
    low = turned[pl.ds(c, ROWS, stride=OWN), :]
    high = turned[pl.ds(CELLS + c, ROWS, stride=OWN), :]
    return jnp.concatenate([low, high], axis=1)


def put_column(turned, c, value):
    turned[pl.ds(c, ROWS, stride=OWN), :] = value[:, :128]
    turned[pl.ds(CELLS + c, ROWS, stride=OWN), :] = value[:, 128:]


def rows_of(turned):
    flat = jnp.concatenate([turned[pl.ds(0, CELLS), :], turned[pl.ds(CELLS, CELLS), :]], axis=1)
    return flat.reshape(ROWS, OWN, CH).astype(BF16)


def fetch(sources, targets, sems):
    copies = [
        pltpu.make_async_copy(source, target, sems.at[i])
        for i, (source, target) in enumerate(zip(sources, targets, strict=True))
    ]
    for copy in copies:
        copy.start()
    return copies


def sea_columns(water):
    eye = lax.broadcasted_iota(jnp.int32, (ROWS, ROWS), 0) == lax.broadcasted_iota(
        jnp.int32, (ROWS, ROWS), 1
    )
    ones = jnp.ones((ROWS, CH), BF16)
    wet = water[...].astype(F32)

    def one(c):
        spread = jnp.where(eye, jnp.broadcast_to(wet[c : c + 1], (ROWS, ROWS)), 0.0)
        return dot(spread.astype(BF16), ones)

    return one


def start_kernel(
    air_far,
    head_far,
    lat_far,
    adj_far,
    water_far,
    sites_far,
    margin_far,
    out,
    to_left,
    to_right,
    air,
    head,
    lat,
    adj,
    water,
    sites,
    margin,
    sems,
    wrapped,
    turned,
):
    copies = fetch(
        (air_far, head_far, lat_far, adj_far, water_far, sites_far, margin_far),
        (air, head, lat, adj, water, sites, margin),
        sems,
    )
    copies[0].wait()
    copies[1].wait()
    fluxes = dot(air[...], head[...])
    wrapped[pl.ds(8, 64), :] = fluxes
    wrapped[pl.ds(0, 8), :] = fluxes[56:64]
    wrapped[pl.ds(72, 8), :] = fluxes[0:8]
    for tile in range(32):
        out[tile] = wrapped[pl.ds(6 + 2 * tile, 8), :].astype(BF16)
    copies[2].wait()
    sides = ((to_left, 0, 0), (to_right, OWN - 2, OWN - 1))
    put_rows(turned, lat[...])
    for ref, first, edge in sides:
        for q in range(2):
            ref[pl.ds(q * ROWS, ROWS), :] = column(turned, first + q).astype(BF16)
    copies[3].wait()
    copies[4].wait()
    put_rows(turned, adj[...])
    sea = sea_columns(water)
    for ref, first, edge in sides:
        ref[pl.ds(2 * ROWS, ROWS), :] = (column(turned, edge) * sea(edge)).astype(BF16)
    copies[5].wait()
    copies[6].wait()
    for ref, first, edge in sides:
        ids = jnp.concatenate([sites[k, first : first + 2, :] for k in range(MARGINS)], axis=0)
        weights = jnp.concatenate([margin[k, first : first + 2, :] for k in range(MARGINS)], axis=0)
        packed = jnp.concatenate([ids, weights], axis=1).astype(F32)
        ref[pl.ds(3 * ROWS, 16), :] = jnp.concatenate(
            [packed, jnp.zeros_like(packed)], axis=0
        ).astype(BF16)


def own_kernel(
    lat_far, adj_far, water, lat_out, cot_out, cot_t, sea_out, inverse, lat, adj, sems, turned, sums
):
    copies = fetch((lat_far, adj_far), (lat, adj), sems)
    sea = sea_columns(water)
    masks = [sea(c) for c in range(OWN)]
    for c in range(OWN):
        sea_out[pl.ds(c * ROWS, ROWS), :] = masks[c][:, :LINK].astype(BF16)
    for half in range(2):
        sums[...] = sum(masks[half * 4 + c][:, :LINK] for c in range(4))
        for side in range(2):
            count = sum(sums[pl.ds(4 * side + i, ZS, stride=8), :] for i in range(4))
            inverse[2 * half + side] = 1.0 / jnp.maximum(count, 1.0)
    copies[0].wait()
    put_rows(turned, lat[...])
    for c in range(OWN):
        lat_out[pl.ds(c * ROWS, ROWS), :] = column(turned, c).astype(BF16)
    copies[1].wait()
    put_rows(turned, adj[...])
    for c in range(OWN):
        cot = column(turned, c) * masks[c]
        cot_out[pl.ds(c * ROWS, ROWS), :] = cot.astype(BF16)
        cot_t[:, pl.ds(c * ROWS, ROWS)] = jnp.transpose(cot).astype(BF16)


def weight_kernel(sites, margin, left, right, out):
    place = lax.broadcasted_iota(jnp.int32, (256, ROWS), 0)
    edges = [ref[pl.ds(3 * ROWS, 16), :].astype(F32) for ref in (left, right)]
    for e in range(WIDE):
        total = jnp.zeros((256, ROWS), F32)
        for k in range(MARGINS):
            if 2 <= e < 2 + OWN:
                ids = sites[k, e - 2 : e - 1, :]
                weight = margin[k, e - 2 : e - 1, :].astype(F32)
                shift = 2
            else:
                side, q, shift = (0, e, 0) if e < 2 else (1, e - 2 - OWN, 4)
                row = edges[side][2 * k + q : 2 * k + q + 1]
                ids = row[:, :ROWS].astype(jnp.int32)
                weight = row[:, ROWS:]
            spot = (ids >> 1) * 8 + (ids & 1) + shift
            total = total + jnp.where(place == spot, weight, 0.0)
        out[pl.ds(e * ROWS, ROWS), :] = jnp.transpose(total).astype(BF16)


PAD = ROWS + 16


def clear_pads(ref):
    zeros = jnp.zeros((8, LINK), F32)
    for i in range(ref.shape[0]):
        ref[i, pl.ds(0, 8), :] = zeros
        ref[i, pl.ds(8 + ROWS, 8), :] = zeros


def ocean_kernel(
    core,
    flux,
    weights,
    lat,
    left,
    right,
    cot,
    cot_t,
    drive_far,
    taps_far,
    gain_far,
    widen_far,
    shrink_far,
    keep,
    send,
    mixed,
    forcing,
    xhat,
    rstd,
    back,
    mlp,
    drive,
    taps,
    gain,
    widen,
    shrink,
    sems,
    normed,
    up,
    down,
):
    copies = fetch(
        (drive_far, taps_far, gain_far, widen_far, shrink_far),
        (drive, taps, gain, widen, shrink),
        sems,
    )
    clear_pads(mixed)
    source = jnp.concatenate([flux[...], jnp.ones((256, LINK), BF16)], axis=1)
    both = dot(weights[...], source)
    force = (both[:, :LINK] / both[:, LINK:]).astype(BF16)
    forcing[...] = force[2 * ROWS : 2 * ROWS + CELLS]
    for copy in copies[:3]:
        copy.wait()
    pushed = dot(force, drive[...])
    for e in range(WIDE):
        if e < 2:
            state = left[pl.ds(e * ROWS, ROWS), :]
        elif e < 2 + OWN:
            state = lat[pl.ds((e - 2) * ROWS, ROWS), :]
        else:
            state = right[pl.ds((e - 2 - OWN) * ROWS, ROWS), :]
        value = state.astype(F32) + pushed[e * ROWS : (e + 1) * ROWS]
        value = value.astype(BF16).astype(F32)
        for h in range(2):
            mixed[2 * e + h, pl.ds(8, ROWS), :] = value[:, h * LINK : (h + 1) * LINK]
    tap = taps[...]
    scale = gain[...]

    def forward(n, carry):
        convs = []
        for h in range(2):
            total = None
            for a in range(3):
                for b in range(3):
                    part = (
                        tap[3 * a + b : 3 * a + b + 1, h * LINK : (h + 1) * LINK]
                        * mixed[2 * (n + b) + h, pl.ds(7 + a, ROWS), :]
                    )
                    total = part if total is None else total + part
            convs.append(total)
        mean = jnp.sum(convs[0] + convs[1], axis=1, keepdims=True) * (1.0 / CH)
        centred = [conv - mean for conv in convs]
        squares = centred[0] * centred[0] + centred[1] * centred[1]
        inv = lax.rsqrt(jnp.sum(squares, axis=1, keepdims=True) * (1.0 / CH) + 1e-6)
        hat = jnp.concatenate([c * inv for c in centred], axis=1)
        rows = pl.ds(pl.multiple_of(n * ROWS, ROWS), ROWS)
        xhat[rows, :] = hat
        rstd[rows, :] = jnp.broadcast_to(inv, (ROWS, LINK))
        normed[rows, :] = (hat * scale).astype(BF16)
        return carry

    lax.fori_loop(0, MID, forward, 0)
    for copy in copies[3:]:
        copy.wait()
    norm = normed[...]
    norm_t = jnp.transpose(norm[ROWS : ROWS + CELLS])
    cots = jnp.concatenate(
        [left[pl.ds(2 * ROWS, ROWS), :], cot[...], right[pl.ds(2 * ROWS, ROWS), :]], axis=0
    )
    for j in range(4):
        cols = pl.ds(j * 256, 256)
        pre = dot(norm, widen[:, cols])
        square = pre * pre
        bend = jnp.tanh(pre * (GELU_A + GELU_B * square))
        half = 0.5 * pre
        more = 1.0 + bend
        hidden = (half * more).astype(BF16)[ROWS : ROWS + CELLS]
        slope = 0.5 * more + half * (1.0 - bend * bend) * (GELU_A + 3.0 * GELU_B * square)
        hidden_cot = dot(cots, shrink[cols, :], NT)
        pre_cot = (hidden_cot * slope).astype(BF16)
        up[:, cols] = dot(norm_t, pre_cot[ROWS : ROWS + CELLS])
        down[cols, :] = jnp.transpose(dot(cot_t[...], hidden))
        add_mlp = dot(hidden, shrink[cols, :])
        add_back = dot(pre_cot, widen[:, cols], NT)
        if j == 0:
            mlp[...] = add_mlp
            back[...] = add_back
        else:
            mlp[...] += add_mlp
            back[...] += add_back

    for which, out in ((0, keep), (1, send)):
        side = core[0] if which == 0 else 1 - core[0]
        for xy in range(XY):
            rows_up = up[pl.ds(pl.multiple_of(side * 128 + xy * 8, 8), 8), :]
            rows_down = down[pl.ds(pl.multiple_of(side * 512 + xy * 32, 32), 32), :]
            tiles = [rows_up[:, z * 128 : (z + 1) * 128] for z in range(8)]
            for g in range(4):
                for lane in range(2):
                    tiles.append(rows_down[g * 8 : g * 8 + 8, lane * 128 : lane * 128 + 128])
            out[xy] = jnp.concatenate(tiles, axis=0).astype(out.dtype)


def rest_kernel(
    mixed,
    forcing,
    xhat,
    rstd,
    back,
    mlp,
    cot,
    sea,
    inverse,
    core,
    taps_far,
    gain_far,
    thermal_far,
    succ_out,
    sst_near,
    sst_across,
    adj_out,
    small,
    taps,
    gain,
    thermal,
    sems,
    curve,
    turned,
    sums,
):
    copies = fetch(
        (gain_far, taps_far, thermal_far), (gain, taps, thermal),
        sems,
    )
    clear_pads(curve)
    for copy in copies[:2]:
        copy.wait()
    scale = gain[...]
    tap = taps[...]

    def backward(n, total):
        rows = pl.ds(pl.multiple_of(n * ROWS, ROWS), ROWS)
        normed_cot = back[rows, :]
        hat = xhat[rows, :]
        grown = normed_cot * scale
        mean = jnp.mean(grown, axis=1, keepdims=True)
        along = jnp.mean(grown * hat, axis=1, keepdims=True)
        inv = rstd[rows, :]
        for h in range(2):
            part = slice(h * LINK, (h + 1) * LINK)
            curve[2 * n + h, pl.ds(8, ROWS), :] = inv * (grown[:, part] - mean - hat[:, part] * along)
        inside = jnp.logical_and(n >= 1, n <= OWN)
        product = jnp.sum((normed_cot * hat).reshape(ROWS // 8, 8, CH), axis=0)
        return total + jnp.where(inside, product, 0.0)

    gain_sum = lax.fori_loop(0, MID, backward, jnp.zeros((8, CH), F32))
    gain_grad = jnp.sum(gain_sum, axis=0, keepdims=True)
    for copy in copies[2:]:
        copy.wait()

    def eightfold(x):
        return jnp.sum(x.reshape(ROWS // 8, 8, LINK), axis=0)

    tap_grads = [[jnp.zeros((8, LINK), F32) for _ in range(9)] for _ in range(2)]
    for c in range(OWN):
        halves = []
        for h in range(2):
            lanes = slice(h * LINK, (h + 1) * LINK)
            moved = [curve[2 * (c + 1) + h, pl.ds(9 - a, ROWS), :] for a in range(3)]
            around = [mixed[2 * (c + 1 + b) + h, pl.ds(8, ROWS), :] for b in range(3)]
            for a in range(3):
                for b in range(3):
                    tap_grads[h][3 * a + b] += eightfold(moved[a] * around[b])
            total = cot[pl.ds(c * ROWS, ROWS), lanes].astype(F32)
            for b in range(3):
                for a in range(3):
                    near = moved[a] if b == 1 else curve[2 * (c + 2 - b) + h, pl.ds(9 - a, ROWS), :]
                    total = total + tap[3 * a + b : 3 * a + b + 1, lanes] * near
            halves.append(total)
        value = jnp.concatenate(halves, axis=1).astype(BF16)
        put_column(turned, c, value.astype(F32))
        part = dot(forcing[pl.ds(c * ROWS, ROWS), :], value, TN)
        force_grad = part if c == 0 else force_grad + part
    adj_out[...] = rows_of(turned)

    rest = jnp.concatenate(
        [
            jnp.concatenate(
                [jnp.sum(tap_grads[h][t], axis=0, keepdims=True) for h in range(2)], axis=1
            )
            for t in range(9)
        ]
        + [gain_grad],
        axis=0,
    )
    for xy in range(XY):
        rows = force_grad[xy * 8 : xy * 8 + 8]
        tail = jnp.zeros((8, LINK), F32)
        if xy < 10:
            row = rest[xy : xy + 1]
            tail = jnp.concatenate([row[:, :128], row[:, 128:], jnp.zeros((6, LINK), F32)], axis=0)
        small[xy] = jnp.concatenate([rows[:, :128], rows[:, 128:], tail], axis=0)

    fine = [None, None]
    for c in range(OWN):
        mask = sea[pl.ds(c * ROWS, ROWS), :].astype(F32)
        state = [
            mask * (mixed[2 * (c + 2) + h, pl.ds(8, ROWS), :] + mlp[pl.ds(c * ROWS, ROWS), h * LINK : (h + 1) * LINK])
            for h in range(2)
        ]
        value = jnp.concatenate(state, axis=1).astype(BF16)
        put_column(turned, c, value.astype(F32))
        part = dot(value, thermal[...])
        fine[c // 4] = part if c % 4 == 0 else fine[c // 4] + part
    succ_out[...] = rows_of(turned)
    for half in range(2):
        sums[...] = fine[half]
        for side, out in ((core[0], sst_near), (1 - core[0], sst_across)):
            coarse = sum(sums[pl.ds(4 * side + i, ZS, stride=8), :] for i in range(4))
            out[half] = (coarse * inverse[2 * half + side]).astype(BF16)


def core_sum_kernel(keep, got, small, out):
    for xy in range(XY):
        out[xy, pl.ds(0, BIG), :] = (keep[xy] + got[xy].astype(F32)).astype(BF16)
        rest = small[xy]
        out[xy, pl.ds(BIG, 16), :] = rest[:16].astype(BF16)
        out[xy, pl.ds(BIG + 16, 8), :] = rest[16:].astype(BF16)


def xy_sum_kernel(got, near, across, out):
    total = got[0].astype(F32)
    for xy in range(1, XY):
        total = total + got[xy].astype(F32)
    row = lax.broadcasted_iota(jnp.int32, (8, LINK), 0)
    surface = [ref[half].astype(F32) for ref in (near, across) for half in range(2)]
    for z in range(ZS):
        rows = [total[BIG + z : BIG + z + 1]]
        rows.append(total[BIG + 16 + z : BIG + 17 + z] if z < 2 else jnp.zeros((1, LINK), F32))
        rows += [values[z : z + 1] for values in surface]
        lower = jnp.zeros((8, LINK), F32)
        for i, values in enumerate(rows):
            lower = jnp.where(row == i, jnp.broadcast_to(values, (8, LINK)), lower)
        out[z] = jnp.concatenate([total[z * 8 : z * 8 + 8], lower], axis=0).astype(BF16)


def z_sum_kernel(factor, core, got, out, sst):
    total = got[0].astype(F32)
    for z in range(1, ZS):
        total = total + got[z].astype(F32)
    value = (total * factor).astype(BF16)
    for z in range(ZS):
        out[z] = value
    own_first = core[0] == 0
    blocks = []
    for z in range(ZS):
        near, across = got[z, 8:16, :].astype(F32)[2:4], got[z, 8:16, :].astype(F32)[4:6]
        blocks.append(jnp.where(own_first, near, across))
        blocks.append(jnp.where(own_first, across, near))
    sst[...] = jnp.concatenate(blocks, axis=0).astype(BF16)


def spread_kernel(got, out):
    pieces = [got[z].astype(F32) for z in range(ZS)]
    big = jnp.concatenate([p[:8] for p in pieces], axis=0)
    force = jnp.concatenate([p[8:9] for p in pieces], axis=0)
    rest = jnp.concatenate([p[9:10] for p in pieces[:8]], axis=0)
    value = jnp.concatenate([big, force, rest], axis=0).astype(BF16)
    for xy in range(XY):
        out[xy] = value


def final_kernel(core, mine, other, up_out, down_out, force_out, conv_out, gain_out):
    for which, ref in ((0, mine), (1, other)):
        side = core[0] if which == 0 else 1 - core[0]
        ups, downs = [], []
        for xy in range(XY):
            block = ref[xy, pl.ds(0, BIG), :].astype(F32)
            tiles = [block[z * 8 : z * 8 + 8] for z in range(ZS)]
            ups.append(jnp.concatenate(tiles[:8], axis=1))
            for g in range(4):
                downs.append(jnp.concatenate(tiles[8 + 2 * g : 10 + 2 * g], axis=1))
        up_out[pl.ds(pl.multiple_of(side * 128, 128), 128), :] = jnp.concatenate(
            ups, axis=0
        ).astype(BF16)
        down_out[pl.ds(pl.multiple_of(side * 512, 512), 512), :] = jnp.concatenate(
            downs, axis=0
        ).astype(BF16)
    rows, rest = [], []
    for xy in range(XY):
        tail = mine[xy, pl.ds(BIG, 24), :].astype(F32) + other[xy, pl.ds(BIG, 24), :].astype(F32)
        rows.append(jnp.concatenate([tail[:8], tail[8:16]], axis=1))
        if xy < 10:
            rest.append(jnp.concatenate([tail[16:17], tail[17:18]], axis=1))
    force_out[...] = jnp.concatenate(rows, axis=0).astype(BF16)
    conv_out[...] = jnp.concatenate(rest[:9], axis=0).astype(BF16)
    gain_out[...] = rest[9].astype(BF16)


def body(
    air,
    head,
    lat,
    drive,
    taps,
    gain,
    widen,
    shrink,
    thermal,
    sites,
    margin,
    water,
    adj,
):
    core = lax.axis_index(CORE).astype(jnp.int32).reshape(1)
    sites_t = jnp.transpose(sites, (0, 2, 1))
    margin_t = jnp.transpose(margin, (0, 2, 1))
    water_t = jnp.transpose(water)
    fluxes, to_left, to_right = call(
        start_kernel,
        (shape(32, 8, LINK), shape(HALO, CH), shape(HALO, CH)),
        [
            pltpu.VMEM((64, air.shape[-1]), BF16),
            pltpu.VMEM(head.shape, BF16),
            pltpu.VMEM((ROWS, OWN, CH), BF16),
            pltpu.VMEM((ROWS, OWN, CH), BF16),
            pltpu.VMEM((OWN, ROWS), jnp.int32),
            pltpu.VMEM((MARGINS, OWN, ROWS), jnp.int32),
            pltpu.VMEM((MARGINS, OWN, ROWS), jnp.int32),
            pltpu.SemaphoreType.DMA((7,)),
            pltpu.VMEM((80, LINK), F32),
            pltpu.VMEM((2 * CELLS, LINK), F32),
        ],
        limit=56,
        moved=2_000_000,
        far=range(7),
    )(air.reshape(64, -1), head, lat[0], adj[0], water_t, sites_t, margin_t)
    ring = [(i, (i + 1) % 32) for i in range(32)]
    left = lax.ppermute(to_right, TILE, ring)
    right = lax.ppermute(to_left, TILE, [(b, a) for a, b in ring])
    flux_in = lax.all_to_all(fluxes, TILE, 0, 0, tiled=True)
    lat_own, cot, cot_t, sea, inverse = call(
        own_kernel,
        (
            held(CELLS, CH),
            held(CELLS, CH),
            held(CH, CELLS),
            held(CELLS, LINK),
            held(4, ROWS // 8, LINK, dtype=F32),
        ),
        [
            pltpu.VMEM((ROWS, OWN, CH), BF16),
            pltpu.VMEM((ROWS, OWN, CH), BF16),
            pltpu.SemaphoreType.DMA((2,)),
            pltpu.VMEM((2 * CELLS, LINK), F32),
            pltpu.VMEM((ROWS, LINK), F32),
        ],
        moved=4_000_000,
        far=(0, 1),
    )(lat[0], adj[0], water_t)
    weights = call(weight_kernel, held(WIDE * ROWS, 256), moved=1_000_000)(
        sites_t, margin_t, left, right
    )
    gain_row = gain.reshape(1, CH)
    keep, send, mixed, forcing, xhat, rstd, back, mlp = call(
        ocean_kernel,
        (
            held(XY, BIG, LINK, dtype=F32),
            held(XY, BIG, LINK),
            held(2 * WIDE, PAD, LINK, dtype=F32),
            held(CELLS, LINK),
            held(MID * ROWS, CH, dtype=F32),
            held(MID * ROWS, LINK, dtype=F32),
            held(MID * ROWS, CH, dtype=F32),
            held(CELLS, CH, dtype=F32),
        ),
        [
            pltpu.VMEM((LINK, CH), BF16),
            pltpu.VMEM((9, CH), F32),
            pltpu.VMEM((1, CH), F32),
            pltpu.VMEM((CH, HID), BF16),
            pltpu.VMEM((HID, CH), BF16),
            pltpu.SemaphoreType.DMA((5,)),
            pltpu.VMEM((MID * ROWS, CH), BF16),
            pltpu.VMEM((CH, HID), F32),
            pltpu.VMEM((HID, CH), F32),
        ],
        limit=36,
        flops=4_000_000_000,
        moved=10_000_000,
        smem=(0,),
        far=range(8, 13),
    )(
        core,
        flux_in.reshape(256, LINK),
        weights,
        lat_own,
        left,
        right,
        cot,
        cot_t,
        drive,
        taps,
        gain_row,
        widen,
        shrink,
    )
    succ, sst_near, sst_across, adj_out, small = call(
        rest_kernel,
        (
            shape(ROWS, OWN, CH),
            held(2, ZS, LINK),
            held(2, ZS, LINK),
            shape(ROWS, OWN, CH),
            held(XY, 24, LINK, dtype=F32),
        ),
        [
            pltpu.VMEM((9, CH), F32),
            pltpu.VMEM((1, CH), F32),
            pltpu.VMEM((CH, LINK), BF16),
            pltpu.SemaphoreType.DMA((3,)),
            pltpu.VMEM((2 * MID, PAD, LINK), F32),
            pltpu.VMEM((2 * CELLS, LINK), F32),
            pltpu.VMEM((ROWS, LINK), F32),
        ],
        limit=24,
        flops=500_000_000,
        moved=8_000_000,
        smem=(9,),
        far=range(10, 13),
    )(mixed, forcing, xhat, rstd, back, mlp, cot, sea, inverse, core, taps, gain_row, thermal)

    swap = [(0, 1), (1, 0)]
    got = lax.ppermute(send, CORE, swap)
    stage = call(core_sum_kernel, held(XY, CHUNK, LINK), moved=2_000_000)(keep, got, small)
    across = lax.ppermute(sst_across, CORE, swap)
    stage = lax.all_to_all(stage, ENS, 0, 0, tiled=True)
    stage = call(xy_sum_kernel, held(ZS, PIECE, LINK), moved=700_000)(stage, sst_near, across)
    stage = lax.all_to_all(stage, Z, 0, 0, tiled=True)
    cells = lax.axis_size(ENS) * lax.axis_size(TILE) * CELLS
    stage, sst_out = call(
        functools.partial(z_sum_kernel, 1.0 / math.sqrt(cells)),
        (held(ZS, PIECE, LINK), shape(64, LINK)),
        moved=100_000,
        smem=(0,),
    )(core, stage)
    stage = lax.all_to_all(stage, Z, 0, 0, tiled=True)
    stage = call(spread_kernel, held(XY, CHUNK, LINK), moved=700_000)(stage)
    stage = lax.all_to_all(stage, ENS, 0, 0, tiled=True)
    other = lax.ppermute(stage, CORE, swap)
    grad_up, grad_down, grad_force, grad_conv, grad_gain = call(
        final_kernel,
        (
            shape(CH, HID),
            shape(HID, CH),
            shape(LINK, CH),
            shape(9, CH),
            shape(1, CH),
        ),
        moved=2_000_000,
        smem=(0,),
    )(core, stage, other)
    return (
        succ[None],
        sst_out.reshape(1, 1, 64, LINK),
        adj_out[None],
        grad_force,
        grad_conv,
        grad_gain.reshape(CH),
        grad_up,
        grad_down,
    )


def solution(mesh):
    finer = Mesh(mesh.devices.reshape(4, 4, 16, 2), (*ENS, *TILE))
    return jax.shard_map(
        body,
        mesh=finer,
        in_specs=(
            P(ENS, TILE, None, None),
            P(),
            P(ENS, None, TILE, None),
            P(),
            P(),
            P(),
            P(),
            P(),
            P(),
            P(None, None, TILE),
            P(None, None, TILE),
            P(None, TILE),
            P(ENS, None, TILE, None),
        ),
        out_specs=(
            P(ENS, None, TILE, None),
            P(ENS, TILE, None, None),
            P(ENS, None, TILE, None),
            P(),
            P(),
            P(),
            P(),
            P(),
        ),
        check_vma=False,
    )
```

time: 386 us -> 125 us (0.32)
  waiting for transfers between devices: 245 us -> 19.5 us
  local copies, waits for them, and re-layouts: 48.4 us -> 0.01 us
  blocking collectives: 0 us -> 44.1 us
  Pallas kernels: 0 us -> 22.1 us
  other arithmetic: 21.3 us -> 0.53 us
  matrix products: 20 us -> 0 us
  starting transfers between devices: 48.4 us -> 37.8 us
    all_to_all x6 -> x2, waiting for transfers between devices: 240 us -> 12.3 us  [the longest x1 8.03 us: body(): stage = lax.all_to_all(stage, ENS, 0, 0, tiled=True)]
    all_to_all x0 -> x3, blocking collectives: none -> 44.1 us  [the longest x2 30.5 us: body(): stage = lax.all_to_all(stage, Z, 0, 0, tiled=True)]
    all_to_all x6 -> x2, starting transfers between devices: 46.5 us -> 23.5 us  [the longest x1 16.8 us: body(): flux_in = lax.all_to_all(fluxes, TILE, 0, 0, tiled=True)]
    pallas_call x0 -> x10, Pallas kernels: none -> 22.1 us  [run(): pl.pallas_call(kernel, out_shape=out_shape, in_specs=[pl.BlockSpec(memory...]
    dot_general x10 -> x0, matrix products: 20 us -> none  [the longest x1 5.26 us: marine_update_kernel(): jnp.dot(hidden, pointwise_shrink_matrix, preferred_element_type=jnp.float32)]
    convert_element_type x12 -> x0, other arithmetic: 14.5 us -> none  [the longest x5 7.55 us: body(): (values * grad_scale).astype(jnp.bfloat16)]
    unnamed x73 -> x6, local copies, waits for them, and re-layouts: 12.8 us -> 0.01 us
    ppermute x4 -> x5, starting transfers between devices: 1.88 us -> 14.3 us  [the longest x1 6.84 us: body(): other = lax.ppermute(stage, CORE, swap)]
  transfers between devices with their start and end apart: 10 -> 7, of which waited for: 9 -> 6; matrix products, arithmetic and copies ran while one was open for 5% -> 0% of each run, Pallas kernels for 0% -> 6%
where the time goes in v1:
time: 125 us
  blocking collectives  44.1 us (35%)
  starting transfers between devices  37.8 us (30%)
  Pallas kernels  22.1 us (18%)
  waiting for transfers between devices  19.5 us (16%)
    all_to_all x2, blocking collectives, body(): stage = lax.all_to_all(stage, Z, 0, 0, tiled=True)  30.5 us
    pallas_call x10, Pallas kernels, run(): pl.pallas_call(kernel, out_shape=out_shape, in_specs=[pl.BlockSpec(memory...  22.1 us
    all_to_all x1, starting transfers between devices, body(): flux_in = lax.all_to_all(fluxes, TILE, 0, 0, tiled=True)  16.8 us
    all_to_all x1, blocking collectives, body(): stage = lax.all_to_all(stage, ENS, 0, 0, tiled=True)  13.6 us
    all_to_all x1, waiting for transfers between devices, body(): stage = lax.all_to_all(stage, ENS, 0, 0, tiled=True)  8.03 us
    ppermute x1, starting transfers between devices, body(): other = lax.ppermute(stage, CORE, swap)  6.84 us
    all_to_all x1, starting transfers between devices, body(): stage = lax.all_to_all(stage, ENS, 0, 0, tiled=True)  6.75 us
    all_to_all x1, waiting for transfers between devices, body(): flux_in = lax.all_to_all(fluxes, TILE, 0, 0, tiled=True)  4.24 us
  transfers between devices with their start and end apart: 7, of which 6 were waited for; matrix products, arithmetic and copies ran while one was open for 0% of the time, Pallas kernels for 6%

profile of v1, /device:TPU:1, one launch (start us, length us, event | category | flops | bytes accessed | tf_op | source)
XLA Modules:
  0.0 124.9 jit_solution(4734465077022991221)
XLA Ops:
  0.7 2.3 %shard_map.188 = (bf16[32,8,128]{2,1,0:T(8,128)(2,1)}, bf16[400,256]{1,0:T(8,128)(2,1)}, bf16[400,256]{1,0:T(8,128)(2,1)}) custom-call(bf16[64,384]{1,0:T(8,128)(2,1)} %bitcast.23, bf16[384,128]{1,0:T(8,128)(2,1)} %head_far.1, bf16[128,8,256]{2,1,0:T(8,128)(2,1)} %bitcast.19, bf16[128,8,256]{2,1,0:T(8,128)(2,1)} %bitcast.21, s32[8,128]{1,0:T(8,128)} %bitcast.17, ...), custom_call_target="tpu_custom_call" | custom-call | bytes 2000000 | tf_op jit(solution)/shard_map/pallas_call | solution.py:48
  3.0 16.8 %all-to-all-start = ((bf16[32,8,128]{2,1,0:T(8,128)(2,1)}), bf16[32,8,128]{2,1,0:T(8,128)(2,1)S(1)}, u32[]{:S(2)}, u32[]{:S(2)}) async-start(bf16[32,8,128]{2,1,0:T(8,128)(2,1)} %get-tuple-element.36), calls=%async_computation | async-start | bytes 131072 | tf_op jit(solution)/shard_map/all_to_all | solution.py:600
  19.7 1.6 %collective-permute-start = (bf16[400,256]{1,0:T(8,128)(2,1)}, bf16[400,256]{1,0:T(8,128)(2,1)S(1)}, u32[]{:S(2)}, u32[]{:S(2)}) collective-permute-start(bf16[400,256]{1,0:T(8,128)(2,1)} %get-tuple-element.37), channel_id=1, source_target_pairs={{0,1},{1,2},{2,3},{3,4},{4,5},{5,6},{6,7},{7,8},{8,9},{9,10},{10,1... | collective-permute-start | bytes 614408 | tf_op jit(solution)/shard_map/ppermute | solution.py:598
  21.4 1.7 %shard_map.190 = (bf16[1024,256]{1,0:T(8,128)(2,1)S(1)}, bf16[1024,256]{1,0:T(8,128)(2,1)S(1)}, bf16[256,1024]{1,0:T(8,128)(2,1)S(1)}, bf16[1024,128]{1,0:T(8,128)(2,1)S(1)}, f32[4,16,128]{2,1,0:T(8,128)S(1)}) custom-call(bf16[128,8,256]{2,1,0:T(8,128)(2,1)} %bitcast.20, bf16[128,8,256]{2,1,0:T(8,128)(2,1)} %bitcast.22, s32[8,128]{1,0:T(8,128)S(1)} %bitcast.18), custom_call_target="tpu_custom_call" | custom-call | bytes 4000000 | tf_op jit(solution)/shard_map/pallas_call | solution.py:48
  23.1 2.8 %collective-permute-done.left = bf16[400,256]{1,0:T(8,128)(2,1)S(1)} collective-permute-done((bf16[400,256]{1,0:T(8,128)(2,1)}, bf16[400,256]{1,0:T(8,128)(2,1)S(1)}, u32[]{:S(2)}, u32[]{:S(2)}) %collective-permute-start) | collective-permute-done | bytes 204832 | tf_op jit(solution)/shard_map/ppermute | solution.py:598
  25.9 1.9 %collective-permute-done.1.right = bf16[400,256]{1,0:T(8,128)(2,1)S(1)} collective-permute-done((bf16[400,256]{1,0:T(8,128)(2,1)}, bf16[400,256]{1,0:T(8,128)(2,1)S(1)}, u32[]{:S(2)}, u32[]{:S(2)}) %collective-permute-start.1) | collective-permute-done | bytes 204832 | tf_op jit(solution)/shard_map/ppermute | solution.py:599
  27.8 0.8 shard_map.189.weights
  28.6 4.2 %all-to-all-done = bf16[32,8,128]{2,1,0:T(8,128)(2,1)S(1)} async-done(((bf16[32,8,128]{2,1,0:T(8,128)(2,1)}), bf16[32,8,128]{2,1,0:T(8,128)(2,1)S(1)}, u32[]{:S(2)}, u32[]{:S(2)}) %all-to-all-start) | async-done | bytes 65568 | tf_op jit(solution)/shard_map/all_to_all | solution.py:600
  32.8 9.6 %shard_map.191 = (f32[16,128,128]{2,1,0:T(8,128)S(1)}, bf16[16,128,128]{2,1,0:T(8,128)(2,1)S(1)}, f32[24,144,128]{2,1,0:T(8,128)S(1)}, bf16[1024,128]{1,0:T(8,12...) custom-call(s32[1]{0:T(128)} %bitcast.core, ...), custom_call_target="tpu_custom_call" | custom-call | flops 4000000000 | bytes 10000000 | tf_op jit(solution)/shard_map/pallas_call | solution.py:48
  42.5 3.6 %collective-permute-start.2 = (bf16[16,128,128]{2,1,0:T(8,128)(2,1)S(1)}, bf16[16,128,128]{2,1,0:T(8,128)(2,1)S(1)}, u32[]{:S(2)}, u32[]{:S(2)}) collective-permute-start(bf16[16,128,128]{2,1,0:T(8,128)(2,1)S(1)} %get-tuple-element.52), channel_id=1, source_target_pairs={{0,1},{1,0},{2,3},{3,2},{4,5},{5,4},{6,7},{7,6},{8,9},{9,8},{10,11... | collective-permute-start | bytes 1572872 | tf_op jit(solution)/shard_map/ppermute | solution.py:693
  46.1 5.0 %shard_map.192 = (bf16[128,8,256]{2,1,0:T(8,128)(2,1)}, bf16[2,16,128]{2,1,0:T(8,128)(2,1)S(1)}, bf16[2,16,128]{2,1,0:T(8,128)(2,1)S(1)}, bf16[128,8,256]{2,1,0:T(8,128)(2,1)}, f32[16,24,128]{2,1,0:T(8,128)S(1)}) custom-call(f32[24,144,128]{2,1,0:T(8,128)S(1)} %get-tuple-element.42.mixed, bf16[1024,128]{1,0:T(8,128)(2,1)S(1)} %get-tuple-element.43.forcing, ...), custom_call_target="tpu_custom_call" | custom-call | flops 500000000 | bytes 8000000 | tf_op jit(solution)/shard_map/pallas_call | solution.py:48
  51.1 0.9 shard_map.193
  52.0 6.8 %all-to-all-start.1 = ((bf16[16,152,128]{2,1,0:T(8,128)(2,1)}), bf16[16,152,128]{2,1,0:T(8,128)(2,1)S(1)}, u32[]{:S(2)}, u32[]{:S(2)}) async-start(bf16[16,152,128]{2,1,0:T(8,128)(2,1)} %shard_map.193), calls=%async_computation.1 | async-start | bytes 1245184 | tf_op jit(solution)/shard_map/all_to_all | solution.py:696
  58.8 2.2 %collective-permute-start.3 = (bf16[2,16,128]{2,1,0:T(8,128)(2,1)S(1)}, bf16[2,16,128]{2,1,0:T(8,128)(2,1)S(1)}, u32[]{:S(2)}, u32[]{:S(2)}) collective-permute-start(bf16[2,16,128]{2,1,0:T(8,128)(2,1)S(1)} %get-tuple-element.55), channel_id=1, source_target_pairs={{0,1},{1,0},{2,3},{3,2},{4,5},{5,4},{6,7},{7,6},{8,9},{9,8},{10,11... | collective-permute-start | bytes 24584 | tf_op jit(solution)/shard_map/ppermute | solution.py:695
  61.0 0.9 collective-permute-done.3.across
  61.9 8.0 %all-to-all-done.1.got = bf16[16,152,128]{2,1,0:T(8,128)(2,1)S(1)} async-done(((bf16[16,152,128]{2,1,0:T(8,128)(2,1)}), bf16[16,152,128]{2,1,0:T(8,128)(2,1)S(1)}, u32[]{:S(2)}, u32[]{:S(2)}) %all-to-all-start.1) | async-done | bytes 622624 | tf_op jit(solution)/shard_map/all_to_all | solution.py:696
  70.0 16.1 %all_to_all.25.got = bf16[16,16,128]{2,1,0:T(8,128)(2,1)S(1)} all-to-all(bf16[16,16,128]{2,1,0:T(8,128)(2,1)S(1)} %shard_map.194), channel_id=1, replica_groups=mesh['ens_0'=4,'ens_1'=4,'tile_0'=16,'tile_1'=2] {'tile_0'}, dimensions={0} | all-to-all | bytes 131072 | tf_op jit(solution)/shard_map/all_to_all | solution.py:698
  86.1 0.6 shard_map.195
  86.8 14.4 %all_to_all.26.got = bf16[16,16,128]{2,1,0:T(8,128)(2,1)S(1)} all-to-all(bf16[16,16,128]{2,1,0:T(8,128)(2,1)S(1)} %get-tuple-element.58), channel_id=1, replica_groups=mesh['ens_0'=4,'ens_1'=4,'tile_0'=16,'tile_1'=2] {'tile_0'}, dimensions={0} | all-to-all | bytes 131072 | tf_op jit(solution)/shard_map/all_to_all | solution.py:706
  101.2 13.6 %all_to_all.27.mine = bf16[16,152,128]{2,1,0:T(8,128)(2,1)S(1)} all-to-all(bf16[16,152,128]{2,1,0:T(8,128)(2,1)S(1)} %shard_map.196), channel_id=1, replica_groups=mesh['ens_0'=4,'ens_1'=4,'tile_0'=16,'tile_1'=2] {'ens_0','ens_1'}, dimensions={0} | all-to-all | bytes 1245184 | tf_op jit(solution)/shard_map/all_to_all | solution.py:708
  114.8 6.8 %collective-permute-start.4 = (bf16[16,152,128]{2,1,0:T(8,128)(2,1)S(1)}, bf16[16,152,128]{2,1,0:T(8,128)(2,1)S(1)}, u32[]{:S(2)}, u32[]{:S(2)}) collective-permute-start(bf16[16,152,128]{2,1,0:T(8,128)(2,1)S(1)} %all_to_all.27.mine), channel_id=1, source_target_pairs={{0,1},{1,0},{2,3},{3,2},{4,5},{5,4},{6,7},{7,6},{8,9},{9,8},{10,11... | collective-permute-start | bytes 1867784 | tf_op jit(solution)/shard_map/ppermute | solution.py:709
  121.7 1.7 %collective-permute-done.4.other = bf16[16,152,128]{2,1,0:T(8,128)(2,1)S(1)} collective-permute-done((bf16[16,152,128]{2,1,0:T(8,128)(2,1)S(1)}, bf16[16,152,128]{2,1,0:T(8,128)(2,1)S(1)}, u32[]{:S(2)}, u32[]{:S(2)}) %collective-permute-start.4) | collective-permute-done | bytes 622624 | tf_op jit(solution)/shard_map/ppermute | solution.py:709
  123.3 1.1 shard_map.197
  124.4 0.5 reduce
  (10 shorter events, 0.2 us)
Async XLA Ops:
  0.6 20.8 %copy-start.2 = (s32[128,8]{0,1:T(8,128)S(1)}, s32[128,8]{0,1:T(8,128)}, u32[]{:S(2)}) copy-start(s32[128,8]{0,1:T(8,128)} %param.24) | copy-start | bytes 12292
  0.6 27.2 %copy-start.1 = (s32[4,128,8]{1,2,0:T(8,128)S(1)}, s32[4,128,8]{1,2,0:T(8,128)}, u32[]{:S(2)}) copy-start(s32[4,128,8]{1,2,0:T(8,128)} %param.23) | copy-start | bytes 49156
  0.7 27.2 %copy-start = (s32[4,128,8]{1,2,0:T(8,128)S(1)}, s32[4,128,8]{1,2,0:T(8,128)}, u32[]{:S(2)}) copy-start(s32[4,128,8]{1,2,0:T(8,128)} %param.22) | copy-start | bytes 49156
  3.0 29.9 %all-to-all-start = ((bf16[32,8,128]{2,1,0:T(8,128)(2,1)}), bf16[32,8,128]{2,1,0:T(8,128)(2,1)S(1)}, u32[]{:S(2)}, u32[]{:S(2)}) async-start(bf16[32,8,128]{2,1,0:T(8,128)(2,1)} %get-tuple-element.36), calls=%async_computation | async-start | bytes 131072 | tf_op jit(solution)/shard_map/all_to_all | solution.py:600
  19.7 6.1 %collective-permute-start = (bf16[400,256]{1,0:T(8,128)(2,1)}, bf16[400,256]{1,0:T(8,128)(2,1)S(1)}, u32[]{:S(2)}, u32[]{:S(2)}) collective-permute-start(bf16[400,256]{1,0:T(8,128)(2,1)} %get-tuple-element.37), channel_id=1, source_target_pairs={{0,1},{1,2},{2,3},{3,4},{4,5},{5,6},{6,7},{7,8},{8,9},{9,10},{10,1... | collective-permute-start | bytes 614408 | tf_op jit(solution)/shard_map/ppermute | solution.py:598
  21.4 6.4 %collective-permute-start.1 = (bf16[400,256]{1,0:T(8,128)(2,1)}, bf16[400,256]{1,0:T(8,128)(2,1)S(1)}, u32[]{:S(2)}, u32[]{:S(2)}) collective-permute-start(bf16[400,256]{1,0:T(8,128)(2,1)} %get-tuple-element.38), channel_id=1, source_target_pairs={{1,0},{2,1},{3,2},{4,3},{5,4},{6,5},{7,6},{8,7},{9,8},{10,9},{11,1... | collective-permute-start | bytes 614408 | tf_op jit(solution)/shard_map/ppermute | solution.py:599
  42.5 8.6 %collective-permute-start.2 = (bf16[16,128,128]{2,1,0:T(8,128)(2,1)S(1)}, bf16[16,128,128]{2,1,0:T(8,128)(2,1)S(1)}, u32[]{:S(2)}, u32[]{:S(2)}) collective-permute-start(bf16[16,128,128]{2,1,0:T(8,128)(2,1)S(1)} %get-tuple-element.52), channel_id=1, source_target_pairs={{0,1},{1,0},{2,3},{3,2},{4,5},{5,4},{6,7},{7,6},{8,9},{9,8},{10,11... | collective-permute-start | bytes 1572872 | tf_op jit(solution)/shard_map/ppermute | solution.py:693
  52.0 17.9 %all-to-all-start.1 = ((bf16[16,152,128]{2,1,0:T(8,128)(2,1)}), bf16[16,152,128]{2,1,0:T(8,128)(2,1)S(1)}, u32[]{:S(2)}, u32[]{:S(2)}) async-start(bf16[16,152,128]{2,1,0:T(8,128)(2,1)} %shard_map.193), calls=%async_computation.1 | async-start | bytes 1245184 | tf_op jit(solution)/shard_map/all_to_all | solution.py:696
  58.8 3.1 %collective-permute-start.3 = (bf16[2,16,128]{2,1,0:T(8,128)(2,1)S(1)}, bf16[2,16,128]{2,1,0:T(8,128)(2,1)S(1)}, u32[]{:S(2)}, u32[]{:S(2)}) collective-permute-start(bf16[2,16,128]{2,1,0:T(8,128)(2,1)S(1)} %get-tuple-element.55), channel_id=1, source_target_pairs={{0,1},{1,0},{2,3},{3,2},{4,5},{5,4},{6,7},{7,6},{8,9},{9,8},{10,11... | collective-permute-start | bytes 24584 | tf_op jit(solution)/shard_map/ppermute | solution.py:695
  114.8 8.5 %collective-permute-start.4 = (bf16[16,152,128]{2,1,0:T(8,128)(2,1)S(1)}, bf16[16,152,128]{2,1,0:T(8,128)(2,1)S(1)}, u32[]{:S(2)}, u32[]{:S(2)}) collective-permute-start(bf16[16,152,128]{2,1,0:T(8,128)(2,1)S(1)} %all_to_all.27.mine), channel_id=1, source_target_pairs={{0,1},{1,0},{2,3},{3,2},{4,5},{5,4},{6,7},{7,6},{8,9},{9,8},{10,11... | collective-permute-start | bytes 1867784 | tf_op jit(solution)/shard_map/ppermute | solution.py:709

commit v2 on v1

v2 whole, which is shorter than its diff:
```python
import functools
import math

import jax
import jax.numpy as jnp
from jax import lax
from jax.experimental import pallas as pl
from jax.experimental.pallas import tpu as pltpu
from jax.sharding import Mesh
from jax.sharding import PartitionSpec as P

F32 = jnp.float32
BF16 = jnp.bfloat16
ENS = ("ens_0", "ens_1")
TILE = ("far", "near", "core")
GROUP = (*ENS, "near")

ROWS = 128
OWN = 8
CH = 256
HID = 1024
LINK = 128
MARGINS = 4
WIDE = OWN + 4
MID = OWN + 2
HALO = 3 * ROWS + 16
CHUNKS = 32
FARS = 8
BIG = 64
CHUNK = 80
BLOCK = 64
PIECE = 96
GELU_A = math.sqrt(2.0 / math.pi)
GELU_B = GELU_A * 0.044715


def call(kernel, out_shape, scratch=(), limit=16, flops=0, moved=0, smem=(), far=()):
    def run(*args):
        args = [
            pltpu.with_memory_space_constraint(arg, pltpu.HBM) if i in far else arg
            for i, arg in enumerate(args)
        ]

        def space(i):
            if i in smem:
                return pltpu.SMEM
            return pltpu.HBM if i in far else pltpu.VMEM

        return pl.pallas_call(
            kernel,
            out_shape=out_shape,
            in_specs=[pl.BlockSpec(memory_space=space(i)) for i in range(len(args))],
            out_specs=jax.tree.map(lambda _: pl.BlockSpec(memory_space=pltpu.VMEM), out_shape),
            scratch_shapes=list(scratch),
            compiler_params=pltpu.CompilerParams(vmem_limit_bytes=limit * 2**20),
            cost_estimate=pl.CostEstimate(flops=flops, bytes_accessed=moved, transcendentals=0),
        )(*args)

    return run


def shape(*dims, dtype=BF16):
    return jax.ShapeDtypeStruct(dims, dtype)


def held(*dims, dtype=BF16):
    return pltpu.VMEM(dims, dtype)


def dot(a, b, contract=((1,), (0,))):
    return lax.dot_general(a, b, (contract, ((), ())), preferred_element_type=F32)


NT = ((1,), (1,))
TN = ((0,), (0,))


CELLS = ROWS * OWN


def put_rows(turned, value):
    flat = value.astype(F32).reshape(CELLS, CH)
    turned[pl.ds(0, CELLS), :] = flat[:, :128]
    turned[pl.ds(CELLS, CELLS), :] = flat[:, 128:]


def column(turned, c):
    low = turned[pl.ds(c, ROWS, stride=OWN), :]
    high = turned[pl.ds(CELLS + c, ROWS, stride=OWN), :]
    return jnp.concatenate([low, high], axis=1)


def put_column(turned, c, value):
    turned[pl.ds(c, ROWS, stride=OWN), :] = value[:, :128]
    turned[pl.ds(CELLS + c, ROWS, stride=OWN), :] = value[:, 128:]


def rows_of(turned):
    flat = jnp.concatenate([turned[pl.ds(0, CELLS), :], turned[pl.ds(CELLS, CELLS), :]], axis=1)
    return flat.reshape(ROWS, OWN, CH).astype(BF16)


def fetch(sources, targets, sems):
    copies = [
        pltpu.make_async_copy(source, target, sems.at[i])
        for i, (source, target) in enumerate(zip(sources, targets, strict=True))
    ]
    for copy in copies:
        copy.start()
    return copies


def sea_columns(water):
    eye = lax.broadcasted_iota(jnp.int32, (ROWS, ROWS), 0) == lax.broadcasted_iota(
        jnp.int32, (ROWS, ROWS), 1
    )
    ones = jnp.ones((ROWS, CH), BF16)
    wet = water[...].astype(F32)

    def one(c):
        spread = jnp.where(eye, jnp.broadcast_to(wet[c : c + 1], (ROWS, ROWS)), 0.0)
        return dot(spread.astype(BF16), ones)

    return one


def spots_of(ids, weight, shift):
    place = lax.broadcasted_iota(jnp.int32, (256, ROWS), 0)
    total = jnp.zeros((256, ROWS), F32)
    for k in range(MARGINS):
        spot = (ids[k] >> 1) * 8 + (ids[k] & 1) + shift
        total = total + jnp.where(place == spot, weight[k], 0.0)
    return jnp.transpose(total).astype(BF16)


def start_kernel(
    air_far,
    head_far,
    lat_far,
    adj_far,
    water_far,
    sites_far,
    margin_far,
    out,
    to_left,
    to_right,
    air,
    head,
    lat,
    adj,
    water,
    sites,
    margin,
    sems,
    wrapped,
    turned,
):
    copies = fetch(
        (air_far, head_far, lat_far, adj_far, water_far, sites_far, margin_far),
        (air, head, lat, adj, water, sites, margin),
        sems,
    )
    copies[0].wait()
    copies[1].wait()
    fluxes = dot(air[...], head[...])
    wrapped[pl.ds(8, 64), :] = fluxes
    wrapped[pl.ds(0, 8), :] = fluxes[56:64]
    wrapped[pl.ds(72, 8), :] = fluxes[0:8]
    for tile in range(32):
        out[tile] = wrapped[pl.ds(6 + 2 * tile, 8), :].astype(BF16)
    copies[2].wait()
    sides = ((to_left, 0, 0), (to_right, OWN - 2, OWN - 1))
    put_rows(turned, lat[...])
    for ref, first, edge in sides:
        for q in range(2):
            ref[pl.ds(q * ROWS, ROWS), :] = column(turned, first + q).astype(BF16)
    copies[3].wait()
    copies[4].wait()
    put_rows(turned, adj[...])
    sea = sea_columns(water)
    for ref, first, edge in sides:
        ref[pl.ds(2 * ROWS, ROWS), :] = (column(turned, edge) * sea(edge)).astype(BF16)
    copies[5].wait()
    copies[6].wait()
    for ref, first, edge in sides:
        ids = jnp.concatenate([sites[k, first : first + 2, :] for k in range(MARGINS)], axis=0)
        weights = jnp.concatenate([margin[k, first : first + 2, :] for k in range(MARGINS)], axis=0)
        packed = jnp.concatenate([ids, weights], axis=1).astype(F32)
        ref[pl.ds(3 * ROWS, 16), :] = jnp.concatenate(
            [packed, jnp.zeros_like(packed)], axis=0
        ).astype(BF16)


def own_kernel(
    lat_far,
    adj_far,
    drive_far,
    taps_far,
    gain_far,
    water_far,
    sites_far,
    margin_far,
    lat_out,
    cot_out,
    cot_t,
    sea_out,
    inverse,
    drive,
    taps,
    gain,
    spots,
    lat,
    adj,
    water,
    sites,
    margin,
    sems,
    turned,
    sums,
):
    copies = fetch(
        (sites_far, margin_far, water_far, lat_far, adj_far, drive_far, taps_far, gain_far),
        (sites, margin, water, lat, adj, drive, taps, gain),
        sems,
    )
    for copy in copies[:3]:
        copy.wait()
    for c in range(OWN):
        ids = [sites[k, c : c + 1, :] for k in range(MARGINS)]
        weight = [margin[k, c : c + 1, :].astype(F32) for k in range(MARGINS)]
        spots[pl.ds(c * ROWS, ROWS), :] = spots_of(ids, weight, 2)
    sea = sea_columns(water)
    masks = [sea(c) for c in range(OWN)]
    for c in range(OWN):
        sea_out[pl.ds(c * ROWS, ROWS), :] = masks[c][:, :LINK].astype(BF16)
    for half in range(2):
        sums[...] = sum(masks[half * 4 + c][:, :LINK] for c in range(4))
        for spot in range(4):
            count = sum(sums[pl.ds(4 * spot + i, FARS, stride=16), :] for i in range(4))
            inverse[4 * half + spot] = 1.0 / jnp.maximum(count, 1.0)
    copies[3].wait()
    put_rows(turned, lat[...])
    for c in range(OWN):
        lat_out[pl.ds(c * ROWS, ROWS), :] = column(turned, c).astype(BF16)
    copies[4].wait()
    put_rows(turned, adj[...])
    for c in range(OWN):
        cot = column(turned, c) * masks[c]
        cot_out[pl.ds(c * ROWS, ROWS), :] = cot.astype(BF16)
        cot_t[:, pl.ds(c * ROWS, ROWS)] = jnp.transpose(cot).astype(BF16)
    for copy in copies[5:]:
        copy.wait()


PAD = ROWS + 16


def clear_pads(ref):
    zeros = jnp.zeros((8, LINK), F32)
    for i in range(ref.shape[0]):
        ref[i, pl.ds(0, 8), :] = zeros
        ref[i, pl.ds(8 + ROWS, 8), :] = zeros


def ocean_kernel(
    place,
    flux,
    spots,
    lat,
    left,
    right,
    cot,
    cot_t,
    drive,
    taps,
    gain,
    widen_far,
    shrink_far,
    keep,
    send,
    mixed,
    forcing,
    xhat,
    rstd,
    hidden,
    pre_cot,
    widen,
    shrink,
    sems,
    normed,
    pres,
    cotangents,
    up,
    down,
):
    copies = fetch((widen_far, shrink_far), (widen, shrink), sems)
    clear_pads(mixed)
    outer = []
    for ref, shift in ((left, 0), (right, 4)):
        packed = ref[pl.ds(3 * ROWS, 16), :].astype(F32)
        for q in range(2):
            rows = [packed[2 * k + q : 2 * k + q + 1] for k in range(MARGINS)]
            ids = [row[:, :ROWS].astype(jnp.int32) for row in rows]
            outer.append(spots_of(ids, [row[:, ROWS:] for row in rows], shift))
    weights = jnp.concatenate([*outer[:2], spots[...], *outer[2:]], axis=0)
    source = jnp.concatenate([flux[...], jnp.ones((256, LINK), BF16)], axis=1)
    both = dot(weights, source)
    force = (both[:, :LINK] / both[:, LINK:]).astype(BF16)
    forcing[...] = force[2 * ROWS : 2 * ROWS + CELLS]
    pushed = dot(force, drive[...])
    for e in range(WIDE):
        if e < 2:
            state = left[pl.ds(e * ROWS, ROWS), :]
        elif e < 2 + OWN:
            state = lat[pl.ds((e - 2) * ROWS, ROWS), :]
        else:
            state = right[pl.ds((e - 2 - OWN) * ROWS, ROWS), :]
        value = state.astype(F32) + pushed[e * ROWS : (e + 1) * ROWS]
        value = value.astype(BF16).astype(F32)
        for h in range(2):
            mixed[2 * e + h, pl.ds(8, ROWS), :] = value[:, h * LINK : (h + 1) * LINK]
    tap = taps[...]
    scale = gain[...]

    def forward(n, carry):
        convs = []
        for h in range(2):
            total = None
            for a in range(3):
                for b in range(3):
                    part = (
                        tap[3 * a + b : 3 * a + b + 1, h * LINK : (h + 1) * LINK]
                        * mixed[2 * (n + b) + h, pl.ds(7 + a, ROWS), :]
                    )
                    total = part if total is None else total + part
            convs.append(total)
        mean = jnp.sum(convs[0] + convs[1], axis=1, keepdims=True) * (1.0 / CH)
        centred = [conv - mean for conv in convs]
        squares = centred[0] * centred[0] + centred[1] * centred[1]
        inv = lax.rsqrt(jnp.sum(squares, axis=1, keepdims=True) * (1.0 / CH) + 1e-6)
        hat = jnp.concatenate([c * inv for c in centred], axis=1)
        rows = pl.ds(pl.multiple_of(n * ROWS, ROWS), ROWS)
        xhat[rows, :] = hat
        rstd[rows, :] = jnp.broadcast_to(inv, (ROWS, LINK))
        normed[rows, :] = (hat * scale).astype(BF16)
        return carry

    lax.fori_loop(0, MID, forward, 0, unroll=MID)
    for copy in copies:
        copy.wait()
    norm = normed[...]
    norm_t = jnp.transpose(norm[ROWS : ROWS + CELLS])
    cots = jnp.concatenate(
        [left[pl.ds(2 * ROWS, ROWS), :], cot[...], right[pl.ds(2 * ROWS, ROWS), :]], axis=0
    )
    for j in range(4):
        cols = pl.ds(j * 256, 256)
        pres[j % 2] = dot(norm, widen[:, cols])
        cotangents[j % 2] = dot(cots, shrink[cols, :], NT)
        for first in range(0, MID * ROWS, BLOCK):
            rows = pl.ds(first, BLOCK)
            pre = pres[j % 2, rows, :]
            square = pre * pre
            bend = jnp.tanh(pre * (GELU_A + GELU_B * square))
            half = 0.5 * pre
            more = 1.0 + bend
            if ROWS <= first < ROWS + CELLS:
                hidden[pl.ds(first - ROWS, BLOCK), cols] = (half * more).astype(BF16)
            slope = 0.5 * more + half * (1.0 - bend * bend) * (GELU_A + 3.0 * GELU_B * square)
            pre_cot[rows, cols] = (cotangents[j % 2, rows, :] * slope).astype(BF16)
        up[:, cols] = dot(norm_t, pre_cot[pl.ds(ROWS, CELLS), cols])
        down[cols, :] = jnp.transpose(dot(cot_t[...], hidden[:, cols]))

    def pack(side, out):
        for g in range(CHUNKS):
            rows_up = pl.ds(side * 128 + g // 4 * 16, 16)
            rows_down = pl.ds(side * 512 + g * 16, 16)
            first = g % 4 * 256
            tiles = [up[rows_up, first : first + 128], up[rows_up, first + 128 : first + 256]]
            tiles += [down[rows_down, :128], down[rows_down, 128:]]
            out[g] = jnp.concatenate(tiles, axis=0).astype(out.dtype)

    for side in range(2):

        @pl.when(place[0] == side)
        def _():
            pack(side, keep)
            pack(1 - side, send)


def rest_kernel(
    mixed,
    forcing,
    xhat,
    rstd,
    pre_cot,
    cot,
    taps,
    gain,
    widen,
    hidden,
    shrink,
    sea,
    adj_out,
    succ_out,
    small,
    curve,
    back,
):
    clear_pads(curve)
    back[...] = dot(pre_cot[...], widen[...], NT)
    scale = gain[...]
    tap = taps[...]

    def backward(n, total):
        rows = pl.ds(pl.multiple_of(n * ROWS, ROWS), ROWS)
        normed_cot = back[rows, :]
        hat = xhat[rows, :]
        grown = normed_cot * scale
        mean = jnp.mean(grown, axis=1, keepdims=True)
        along = jnp.mean(grown * hat, axis=1, keepdims=True)
        inv = rstd[rows, :]
        for h in range(2):
            part = slice(h * LINK, (h + 1) * LINK)
            curve[2 * n + h, pl.ds(8, ROWS), :] = inv * (grown[:, part] - mean - hat[:, part] * along)
        inside = jnp.logical_and(n >= 1, n <= OWN)
        product = jnp.sum((normed_cot * hat).reshape(ROWS // 8, 8, CH), axis=0)
        return total + jnp.where(inside, product, 0.0)

    gain_sum = lax.fori_loop(
        0, MID, backward, jnp.zeros((8, CH), F32), unroll=MID
    )
    gain_grad = jnp.sum(gain_sum, axis=0, keepdims=True)

    def eightfold(x):
        return jnp.sum(x.reshape(ROWS // 8, 8, LINK), axis=0)

    tap_grads = [[jnp.zeros((8, LINK), F32) for _ in range(9)] for _ in range(2)]
    for c in range(OWN):
        halves = []
        for h in range(2):
            lanes = slice(h * LINK, (h + 1) * LINK)
            moved = [curve[2 * (c + 1) + h, pl.ds(9 - a, ROWS), :] for a in range(3)]
            around = [mixed[2 * (c + 1 + b) + h, pl.ds(8, ROWS), :] for b in range(3)]
            for a in range(3):
                for b in range(3):
                    tap_grads[h][3 * a + b] += eightfold(moved[a] * around[b])
            total = cot[pl.ds(c * ROWS, ROWS), lanes].astype(F32)
            for b in range(3):
                for a in range(3):
                    near = moved[a] if b == 1 else curve[2 * (c + 2 - b) + h, pl.ds(9 - a, ROWS), :]
                    total = total + tap[3 * a + b : 3 * a + b + 1, lanes] * near
            halves.append(total)
        value = jnp.concatenate(halves, axis=1).astype(BF16)
        adj_out[pl.ds(c * ROWS, ROWS), :] = value
    force_grad = dot(forcing[...], adj_out[...], TN)

    rest = jnp.concatenate(
        [
            jnp.concatenate(
                [jnp.sum(tap_grads[h][t], axis=0, keepdims=True) for h in range(2)], axis=1
            )
            for t in range(9)
        ]
        + [gain_grad],
        axis=0,
    )
    for g in range(CHUNKS):
        lanes = slice(g % 2 * 128, g % 2 * 128 + 128)
        tail = jnp.zeros((8, LINK), F32)
        if g < 20:
            tail = jnp.concatenate([rest[g // 2 : g // 2 + 1, lanes], tail[1:]], axis=0)
        small[g] = jnp.concatenate([force_grad[g // 2 * 8 : g // 2 * 8 + 8, lanes], tail], axis=0)
    mlp = dot(hidden[...], shrink[...])
    for c in range(OWN):
        mask = sea[pl.ds(c * ROWS, ROWS), :].astype(F32)
        for h in range(2):
            lanes = slice(h * LINK, (h + 1) * LINK)
            state = mixed[2 * (c + 2) + h, pl.ds(8, ROWS), :] + mlp[c * ROWS : (c + 1) * ROWS, lanes]
            succ_out[pl.ds(c * ROWS, ROWS), lanes] = (mask * state).astype(BF16)


def state_kernel(
    succ,
    inverse,
    adj,
    place,
    thermal_far,
    succ_out,
    sst_near,
    sst_across,
    adj_out,
    thermal,
    sem,
    turned,
    sums,
):
    wait_for = pltpu.make_async_copy(thermal_far, thermal, sem)
    wait_for.start()
    wait_for.wait()
    fine = [None, None]
    for c in range(OWN):
        value = succ[pl.ds(c * ROWS, ROWS), :]
        put_column(turned, c, value.astype(F32))
        part = dot(value, thermal[...])
        fine[c // 4] = part if c % 4 == 0 else fine[c // 4] + part
    succ_out[...] = rows_of(turned)
    for half in range(2):
        sums[...] = fine[half]
        for across, out in enumerate((sst_near, sst_across)):
            for other in range(2):
                core = jnp.bitwise_xor(place[0], across)
                spot = 2 * jnp.bitwise_xor(place[1], other) + core
                coarse = sum(sums[pl.ds(4 * spot + i, FARS, stride=16), :] for i in range(4))
                out[other, half] = (coarse * inverse[4 * half + spot]).astype(BF16)
    for c in range(OWN):
        put_column(turned, c, adj[pl.ds(c * ROWS, ROWS), :].astype(F32))
    adj_out[...] = rows_of(turned)


def core_sum_kernel(keep, got, small, out):
    for g in range(CHUNKS):
        out[g, pl.ds(0, BIG), :] = (keep[g] + got[g].astype(F32)).astype(BF16)
        out[g, pl.ds(BIG, 16), :] = small[g].astype(BF16)


def group_sum_kernel(got, near, across, out):
    total = got[0].astype(F32)
    for g in range(1, CHUNKS):
        total = total + got[g].astype(F32)
    value = total.astype(BF16)
    row = lax.broadcasted_iota(jnp.int32, (8, LINK), 0)
    surface = [ref[i, half].astype(F32) for i in range(2) for ref in (near, across) for half in range(2)]
    for far in range(FARS):
        lower = jnp.broadcast_to(surface[0][far : far + 1], (8, LINK))
        for i in range(1, 8):
            lower = jnp.where(row == i, jnp.broadcast_to(surface[i][far : far + 1], (8, LINK)), lower)
        out[far, pl.ds(0, CHUNK), :] = value
        out[far, pl.ds(CHUNK, 16), :] = jnp.concatenate([lower, lower], axis=0).astype(BF16)


def far_sum_kernel(factor, got, out, surface):
    total = got[0, pl.ds(0, CHUNK), :].astype(F32)
    for far in range(1, FARS):
        total = total + got[far, pl.ds(0, CHUNK), :].astype(F32)
    value = (total * factor).astype(BF16)
    for g in range(CHUNKS):
        out[g] = value
    for far in range(FARS):
        surface[far] = got[far, pl.ds(CHUNK, 16), :]


def final_kernel(place, mine, other, kept, moved, up_out, down_out, force_out, conv_out, gain_out, sst):
    def unpack(side, ref):
        for row in range(8):
            tiles = [ref[4 * row + i, pl.ds(t * 16, 16), :] for i in range(4) for t in range(2)]
            up_out[pl.ds(side * 128 + row * 16, 16), :] = jnp.concatenate(tiles, axis=1)
        for g in range(CHUNKS):
            tiles = [ref[g, pl.ds(32 + t * 16, 16), :] for t in range(2)]
            down_out[pl.ds(side * 512 + g * 16, 16), :] = jnp.concatenate(tiles, axis=1)

    for side in range(2):

        @pl.when(place[0] == side)
        def _():
            unpack(side, mine)
            unpack(1 - side, other)

    blocks = []
    for far in range(FARS):
        own, came = kept[far].astype(F32)[0:4], moved[far].astype(F32)[4:8]
        pairs = []
        for part in (own, came):
            swapped = jnp.concatenate([part[2:4], part[0:2]], axis=0)
            pairs.append(jnp.where(place[0] == 0, part, swapped))
        first = jnp.where(place[1] == 0, pairs[0], pairs[1])
        second = jnp.where(place[1] == 0, pairs[1], pairs[0])
        blocks += [first, second]
    sst[...] = jnp.concatenate(blocks, axis=0).astype(BF16)

    rows, rest = [], []
    for pair in range(CHUNKS // 2):
        tails = [
            mine[2 * pair + i, pl.ds(BIG, 16), :].astype(F32)
            + other[2 * pair + i, pl.ds(BIG, 16), :].astype(F32)
            for i in range(2)
        ]
        rows.append(jnp.concatenate([tail[:8] for tail in tails], axis=1))
        if pair < 10:
            rest.append(jnp.concatenate([tail[8:9] for tail in tails], axis=1))
    force_out[...] = jnp.concatenate(rows, axis=0).astype(BF16)
    conv_out[...] = jnp.concatenate(rest[:9], axis=0).astype(BF16)
    gain_out[...] = rest[9].astype(BF16).reshape(gain_out.shape)


def body(
    air,
    head,
    lat,
    drive,
    taps,
    gain,
    widen,
    shrink,
    thermal,
    sites,
    margin,
    water,
    adj,
):
    place = jnp.stack([lax.axis_index("core"), lax.axis_index("near")]).astype(jnp.int32)
    sites_t = jnp.transpose(sites, (0, 2, 1))
    margin_t = jnp.transpose(margin, (0, 2, 1))
    water_t = jnp.transpose(water)
    fluxes, to_left, to_right = call(
        start_kernel,
        (shape(32, 8, LINK), shape(HALO, CH), shape(HALO, CH)),
        [
            pltpu.VMEM((64, air.shape[-1]), BF16),
            pltpu.VMEM(head.shape, BF16),
            pltpu.VMEM((ROWS, OWN, CH), BF16),
            pltpu.VMEM((ROWS, OWN, CH), BF16),
            pltpu.VMEM((OWN, ROWS), jnp.int32),
            pltpu.VMEM((MARGINS, OWN, ROWS), jnp.int32),
            pltpu.VMEM((MARGINS, OWN, ROWS), jnp.int32),
            pltpu.SemaphoreType.DMA((7,)),
            pltpu.VMEM((80, LINK), F32),
            pltpu.VMEM((2 * CELLS, LINK), F32),
        ],
        limit=56,
        moved=2_000_000,
        far=range(7),
    )(air.reshape(64, -1), head, lat[0], adj[0], water_t, sites_t, margin_t)
    ring = [(i, (i + 1) % 32) for i in range(32)]
    left = lax.ppermute(to_right, TILE, ring)
    right = lax.ppermute(to_left, TILE, [(b, a) for a, b in ring])
    flux_in = lax.all_to_all(fluxes, TILE, 0, 0, tiled=True)
    gain_row = gain.reshape(1, CH)
    lat_own, cot, cot_t, sea, inverse, drive, taps, gain_row, spots = call(
        own_kernel,
        (
            held(CELLS, CH),
            held(CELLS, CH),
            held(CH, CELLS),
            held(CELLS, LINK),
            held(8, FARS, LINK, dtype=F32),
            held(LINK, CH),
            held(9, CH, dtype=F32),
            held(1, CH, dtype=F32),
            held(CELLS, 256),
        ),
        [
            pltpu.VMEM((ROWS, OWN, CH), BF16),
            pltpu.VMEM((ROWS, OWN, CH), BF16),
            pltpu.VMEM((OWN, ROWS), jnp.int32),
            pltpu.VMEM((MARGINS, OWN, ROWS), jnp.int32),
            pltpu.VMEM((MARGINS, OWN, ROWS), jnp.int32),
            pltpu.SemaphoreType.DMA((8,)),
            pltpu.VMEM((2 * CELLS, LINK), F32),
            pltpu.VMEM((ROWS, LINK), F32),
        ],
        moved=4_000_000,
        far=range(8),
    )(lat[0], adj[0], drive, taps, gain_row, water_t, sites_t, margin_t)
    keep, send, mixed, forcing, xhat, rstd, hidden, pre_cot, widen, shrink = call(
        ocean_kernel,
        (
            held(CHUNKS, BIG, LINK, dtype=F32),
            held(CHUNKS, BIG, LINK),
            held(2 * WIDE, PAD, LINK, dtype=F32),
            held(CELLS, LINK),
            held(MID * ROWS, CH, dtype=F32),
            held(MID * ROWS, LINK, dtype=F32),
            held(CELLS, HID),
            held(MID * ROWS, HID),
            held(CH, HID),
            held(HID, CH),
        ),
        [
            pltpu.SemaphoreType.DMA((2,)),
            pltpu.VMEM((MID * ROWS, CH), BF16),
            pltpu.VMEM((2, MID * ROWS, CH), F32),
            pltpu.VMEM((2, MID * ROWS, CH), F32),
            pltpu.VMEM((CH, HID), F32),
            pltpu.VMEM((HID, CH), F32),
        ],
        limit=24,
        flops=4_000_000_000,
        moved=10_000_000,
        smem=(0,),
        far=(11, 12),
    )(
        place,
        flux_in.reshape(256, LINK),
        spots,
        lat_own,
        left,
        right,
        cot,
        cot_t,
        drive,
        taps,
        gain_row,
        widen,
        shrink,
    )
    adj_turned, succ_turned, small = call(
        rest_kernel,
        (held(CELLS, CH), held(CELLS, CH), held(CHUNKS, 16, LINK, dtype=F32)),
        [
            pltpu.VMEM((2 * MID, PAD, LINK), F32),
            pltpu.VMEM((MID * ROWS, CH), F32),
        ],
        flops=1_000_000_000,
        moved=8_000_000,
    )(mixed, forcing, xhat, rstd, pre_cot, cot, taps, gain_row, widen, hidden, shrink, sea)

    swap = [(0, 1), (1, 0)]
    got = lax.ppermute(send, "core", swap)
    stage = call(core_sum_kernel, held(CHUNKS, CHUNK, LINK), moved=2_000_000)(keep, got, small)
    stage, succ_turned = lax.optimization_barrier((stage, succ_turned))
    stage = lax.all_to_all(stage, GROUP, 0, 0, tiled=True)
    succ, sst_near, sst_across, adj_out = call(
        state_kernel,
        (
            shape(ROWS, OWN, CH),
            held(2, 2, FARS, LINK),
            held(2, 2, FARS, LINK),
            shape(ROWS, OWN, CH),
        ),
        [
            pltpu.VMEM((CH, LINK), BF16),
            pltpu.SemaphoreType.DMA(()),
            pltpu.VMEM((2 * CELLS, LINK), F32),
            pltpu.VMEM((ROWS, LINK), F32),
        ],
        flops=1_000_000_000,
        moved=5_000_000,
        smem=(3,),
        far=(4,),
    )(succ_turned, inverse, adj_turned, place, thermal)
    across = lax.ppermute(sst_across, "core", swap)
    stage = call(group_sum_kernel, held(FARS, PIECE, LINK), moved=700_000)(stage, sst_near, across)
    stage = lax.all_to_all(stage, "far", 0, 0, tiled=True)
    cells = lax.axis_size(ENS) * lax.axis_size(TILE) * CELLS
    stage, surface = call(
        functools.partial(far_sum_kernel, 1.0 / math.sqrt(cells)),
        (held(CHUNKS, CHUNK, LINK), held(FARS, 16, LINK)),
        moved=700_000,
    )(stage)
    stage = lax.all_to_all(stage, GROUP, 0, 0, tiled=True)
    moved = lax.ppermute(surface, "near", swap)
    stage, moved = lax.optimization_barrier((stage, moved))
    other = lax.ppermute(stage, "core", swap)
    grad_up, grad_down, grad_force, grad_conv, grad_gain, sst_out = call(
        final_kernel,
        (
            shape(CH, HID),
            shape(HID, CH),
            shape(LINK, CH),
            shape(9, CH),
            shape(CH),
            shape(64, LINK),
        ),
        moved=2_000_000,
        smem=(0,),
    )(place, stage, other, surface, moved)
    return (
        succ[None],
        sst_out.reshape(1, 1, 64, LINK),
        adj_out[None],
        grad_force,
        grad_conv,
        grad_gain,
        grad_up,
        grad_down,
    )


def solution(mesh):
    finer = Mesh(mesh.devices.reshape(4, 4, 8, 2, 2), (*ENS, *TILE))
    return jax.shard_map(
        body,
        mesh=finer,
        in_specs=(
            P(ENS, TILE, None, None),
            P(),
            P(ENS, None, TILE, None),
            P(),
            P(),
            P(),
            P(),
            P(),
            P(),
            P(None, None, TILE),
            P(None, None, TILE),
            P(None, TILE),
            P(ENS, None, TILE, None),
        ),
        out_specs=(
            P(ENS, None, TILE, None),
            P(ENS, TILE, None, None),
            P(ENS, None, TILE, None),
            P(),
            P(),
            P(),
            P(),
            P(),
        ),
        check_vma=False,
    )
```

time: 125 us -> 116 us (0.928)
  blocking collectives: 44.1 us -> 19.3 us
  starting transfers between devices: 37.8 us -> 45.5 us
  waiting for transfers between devices: 19.5 us -> 26.6 us
    all_to_all x3 -> x1, blocking collectives: 44.1 us -> 19.3 us  [body(): stage = lax.all_to_all(stage, 'far', 0, 0, tiled=True)]
    all_to_all x1 -> x2, starting transfers between devices: 6.75 us -> 11.3 us  [body(): stage = lax.all_to_all(stage, GROUP, 0, 0, tiled=True)]
    all_to_all x1 -> x2, waiting for transfers between devices: 8.03 us -> 11.8 us  [body(): stage = lax.all_to_all(stage, GROUP, 0, 0, tiled=True)]
    ppermute x3 -> x4, waiting for transfers between devices: 2.52 us -> 5.56 us  [the longest x1 2.99 us: body(): moved = lax.ppermute(surface, 'near', swap)]
    ppermute x3 -> x4, starting transfers between devices: 12.7 us -> 15.7 us  [the longest x1 6.6 us: body(): other = lax.ppermute(stage, 'core', swap)]
    pallas_call x10 -> x9, Pallas kernels: 22.1 us -> 23.2 us  [run(): pl.pallas_call(kernel, out_shape=out_shape, in_specs=[pl.BlockSpec(memory...]
  transfers between devices with their start and end apart: 7 -> 9, of which waited for: 6 -> 8; matrix products, arithmetic and copies ran while one was open for 0% -> 0% of each run, Pallas kernels for 6% -> 9%
where the time goes in v2:
time: 116 us; the launch traced here: 115 us
  starting transfers between devices  45.5 us (39%)
  waiting for transfers between devices  26.6 us (23%)
  Pallas kernels  23.2 us (20%)
  blocking collectives  19.3 us (17%)
    pallas_call x9, Pallas kernels, run(): pl.pallas_call(kernel, out_shape=out_shape, in_specs=[pl.BlockSpec(memory...  23.2 us
    all_to_all x1, blocking collectives, body(): stage = lax.all_to_all(stage, 'far', 0, 0, tiled=True)  19.3 us
    all_to_all x1, starting transfers between devices, body(): flux_in = lax.all_to_all(fluxes, TILE, 0, 0, tiled=True)  16.8 us
    all_to_all x2, waiting for transfers between devices, body(): stage = lax.all_to_all(stage, GROUP, 0, 0, tiled=True)  11.8 us
    all_to_all x2, starting transfers between devices, body(): stage = lax.all_to_all(stage, GROUP, 0, 0, tiled=True)  11.3 us
    ppermute x1, starting transfers between devices, body(): other = lax.ppermute(stage, 'core', swap)  6.6 us
    all_to_all x1, waiting for transfers between devices, body(): flux_in = lax.all_to_all(fluxes, TILE, 0, 0, tiled=True)  5.02 us
    ppermute x1, starting transfers between devices, body(): got = lax.ppermute(send, 'core', swap)  3.77 us
  transfers between devices with their start and end apart: 9, of which 8 were waited for; matrix products, arithmetic and copies ran while one was open for 0% of the time, Pallas kernels for 9%

profile of v2, /device:TPU:1, one launch (start us, length us, event | category | flops | bytes accessed | tf_op | source)
XLA Modules:
  0.0 115.4 jit_solution(15935674161560817544)
XLA Ops:
  0.6 2.3 %shard_map.188 = (bf16[32,8,128]{2,1,0:T(8,128)(2,1)}, bf16[400,256]{1,0:T(8,128)(2,1)}, bf16[400,256]{1,0:T(8,128)(2,1)}) custom-call(bf16[64,384]{1,0:T(8,128)(2,1)} %bitcast.22, bf16[384,128]{1,0:T(8,128)(2,1)} %head_far.1, bf16[128,8,256]{2,1,0:T(8,128)(2,1)} %bitcast.14, bf16[128,8,256]{2,1,0:T(8,128)(2,1)} %bitcast.16, s32[8,128]{1,0:T(8,128)} %bitcast.23, ...), custom_call_target="tpu_custom_call" | custom-call | bytes 2000000 | tf_op jit(solution)/shard_map/pallas_call | solution.py:49
  2.9 16.8 %all-to-all-start = ((bf16[32,8,128]{2,1,0:T(8,128)(2,1)}), bf16[32,8,128]{2,1,0:T(8,128)(2,1)S(1)}, u32[]{:S(2)}, u32[]{:S(2)}) async-start(bf16[32,8,128]{2,1,0:T(8,128)(2,1)} %get-tuple-element.49), calls=%async_computation | async-start | bytes 131072 | tf_op jit(solution)/shard_map/all_to_all | solution.py:637
  19.7 1.6 %collective-permute-start = (bf16[400,256]{1,0:T(8,128)(2,1)}, bf16[400,256]{1,0:T(8,128)(2,1)S(1)}, u32[]{:S(2)}, u32[]{:S(2)}) collective-permute-start(bf16[400,256]{1,0:T(8,128)(2,1)} %get-tuple-element.52), channel_id=1, source_target_pairs={{0,1},{1,2},{2,3},{3,4},{4,5},{5,6},{6,7},{7,8},{8,9},{9,10},{10,1... | collective-permute-start | bytes 614408 | tf_op jit(solution)/shard_map/ppermute | solution.py:635
  21.4 2.1 %shard_map.189 = (bf16[1024,256]{1,0:T(8,128)(2,1)S(1)}, bf16[1024,256]{1,0:T(8,128)(2,1)S(1)}, bf16[256,1024]{1,0:T(8,128)(2,1)S(1)}, bf16[1024,128]{1,0:T(8,12...) custom-call(bf16[128,8,256]{2,1,0:T(8,128)(2,1)} %bitcast.15, ...), custom_call_target="tpu_custom_call" | custom-call | bytes 4000000 | tf_op jit(solution)/shard_map/pallas_call | solution.py:49
  23.6 2.2 %collective-permute-done.left = bf16[400,256]{1,0:T(8,128)(2,1)S(1)} collective-permute-done((bf16[400,256]{1,0:T(8,128)(2,1)}, bf16[400,256]{1,0:T(8,128)(2,1)S(1)}, u32[]{:S(2)}, u32[]{:S(2)}) %collective-permute-start) | collective-permute-done | bytes 204832 | tf_op jit(solution)/shard_map/ppermute | solution.py:635
  25.8 1.9 %collective-permute-done.1.right = bf16[400,256]{1,0:T(8,128)(2,1)S(1)} collective-permute-done((bf16[400,256]{1,0:T(8,128)(2,1)}, bf16[400,256]{1,0:T(8,128)(2,1)S(1)}, u32[]{:S(2)}, u32[]{:S(2)}) %collective-permute-start.1) | collective-permute-done | bytes 204832 | tf_op jit(solution)/shard_map/ppermute | solution.py:636
  27.8 5.0 %all-to-all-done = bf16[32,8,128]{2,1,0:T(8,128)(2,1)S(1)} async-done(((bf16[32,8,128]{2,1,0:T(8,128)(2,1)}), bf16[32,8,128]{2,1,0:T(8,128)(2,1)S(1)}, u32[]{:S(2)}, u32[]{:S(2)}) %all-to-all-start) | async-done | bytes 65568 | tf_op jit(solution)/shard_map/all_to_all | solution.py:637
  32.8 7.4 %shard_map.190 = (f32[32,64,128]{2,1,0:T(8,128)S(1)}, bf16[32,64,128]{2,1,0:T(8,128)(2,1)S(1)}, f32[24,144,128]{2,1,0:T(8,128)S(1)}, bf16[1024,128]{1,0:T(8,128)...) custom-call(s32[2]{0:T(128)S(1)} %pad_add_fusion.place, ...), custom_call_target="tpu_custom_call" | custom-call | flops 4000000000 | bytes 10000000 | tf_op jit(solution)/shard_map/pallas_call | solution.py:49
  40.2 3.8 %collective-permute-start.2 = (bf16[32,64,128]{2,1,0:T(8,128)(2,1)S(1)}, bf16[32,64,128]{2,1,0:T(8,128)(2,1)S(1)}, u32[]{:S(2)}, u32[]{:S(2)}) collective-permute-start(bf16[32,64,128]{2,1,0:T(8,128)(2,1)S(1)} %get-tuple-element.60), channel_id=1, source_target_pairs={{0,1},{1,0},{2,3},{3,2},{4,5},{5,4},{6,7},{7,6},{8,9},{9,8},{10,11... | collective-permute-start | bytes 1572872 | tf_op jit(solution)/shard_map/ppermute | solution.py:719
  44.0 5.0 %shard_map.191 = (bf16[1024,256]{1,0:T(8,128)(2,1)S(1)}, bf16[1024,256]{1,0:T(8,128)(2,1)S(1)}, f32[32,16,128]{2,1,0:T(8,128)S(1)}) custom-call(f32[24,144,128]{2,1,0:T(8,128)S(1)} %get-tuple-element.61.mixed, bf16[1024,128]{1,0:T(8,128)(2,1)S(1)} %get-tuple-element.62.forcing, f32[1280,256]{1,0:T(8,128)S(1)} %get-tuple-element.63.xhat, ...), custom_call_target="tpu_custom_call" | custom-call | flops 1000000000 | bytes 8000000 | tf_op jit(solution)/shard_map/pallas_call | solution.py:49
  49.0 0.9 shard_map.192
  49.9 7.0 %all-to-all-start.1 = ((bf16[32,80,128]{2,1,0:T(8,128)(2,1)}), bf16[32,80,128]{2,1,0:T(8,128)(2,1)S(1)}, u32[]{:S(2)}, u32[]{:S(2)}) async-start(bf16[32,80,128]{2,1,0:T(8,128)(2,1)} %shard_map.192), calls=%async_computation.1 | async-start | bytes 1310720 | tf_op jit(solution)/shard_map/all_to_all | solution.py:722
  57.0 2.9 %shard_map.193 = (bf16[128,8,256]{2,1,0:T(8,128)(2,1)}, bf16[2,2,8,128]{3,2,1,0:T(8,128)(2,1)S(1)}, bf16[2,2,8,128]{3,2,1,0:T(8,128)(2,1)S(1)}, bf16[128,8,256]{2,1,0:T(8,128)(2,1)}) custom-call(bf16[1024,256]{1,0:T(8,128)(2,1)S(1)} %get-tuple-element.72.succ, f32[8,8,128]{2,1,0:T(8,128)S(1)} %get-tuple-element.73.inverse, ...), custom_call_target="tpu_custom_call" | custom-call | flops 1000000000 | bytes 5000000 | tf_op jit(solution)/shard_map/pallas_call | solution.py:49
  59.8 2.2 %collective-permute-start.3 = (bf16[2,2,8,128]{3,2,1,0:T(8,128)(2,1)S(1)}, bf16[2,2,8,128]{3,2,1,0:T(8,128)(2,1)S(1)}, u32[]{:S(2)}, u32[]{:S(2)}) collective-permute-start(bf16[2,2,8,128]{3,2,1,0:T(8,128)(2,1)S(1)} %get-tuple-element.78), channel_id=1, source_target_pairs={{0,1},{1,0},{2,3},{3,2},{4,5},{5,4},{6,7},{7,6},{8,9},{9,8},{10,11... | collective-permute-start | bytes 24584 | tf_op jit(solution)/shard_map/ppermute | solution.py:742
  62.9 7.2 %all-to-all-done.1.got = bf16[32,80,128]{2,1,0:T(8,128)(2,1)S(1)} async-done(((bf16[32,80,128]{2,1,0:T(8,128)(2,1)}), bf16[32,80,128]{2,1,0:T(8,128)(2,1)S(1)}, u32[]{:S(2)}, u32[]{:S(2)}) %all-to-all-start.1) | async-done | bytes 655392 | tf_op jit(solution)/shard_map/all_to_all | solution.py:722
  70.3 19.3 %all_to_all.20.got = bf16[8,96,128]{2,1,0:T(8,128)(2,1)S(1)} all-to-all(bf16[8,96,128]{2,1,0:T(8,128)(2,1)S(1)} %shard_map.194), channel_id=1, replica_groups=mesh['ens_0'=4,'ens_1'=4,'far'=8,'near'=2,'core'=2] {'far'}, dimensions={0} | all-to-all | bytes 393216 | tf_op jit(solution)/shard_map/all_to_all | solution.py:744
  89.6 0.9 shard_map.195
  90.5 4.3 %all-to-all-start.3 = ((bf16[32,80,128]{2,1,0:T(8,128)(2,1)}), bf16[32,80,128]{2,1,0:T(8,128)(2,1)S(1)}, u32[]{:S(2)}, u32[]{:S(2)}) async-start(bf16[32,80,128]{2,1,0:T(8,128)(2,1)} %get-tuple-element.79), calls=%async_computation.3 | async-start | bytes 1310720 | tf_op jit(solution)/shard_map/all_to_all | solution.py:751
  94.8 3.1 %collective-permute-start.4 = (bf16[8,16,128]{2,1,0:T(8,128)(2,1)S(1)}, bf16[8,16,128]{2,1,0:T(8,128)(2,1)S(1)}, u32[]{:S(2)}, u32[]{:S(2)}) collective-permute-start(bf16[8,16,128]{2,1,0:T(8,128)(2,1)S(1)} %get-tuple-element.80.kept), channel_id=1, source_target_pairs={{0,2},{2,0},{1,3},{3,1},{4,6},{6,4},{5,7},{7,5},{8,10},{10,8},{9,1... | collective-permute-start | bytes 98312 | tf_op jit(solution)/shard_map/ppermute | solution.py:752
  97.9 3.0 %collective-permute-done.4.moved = bf16[8,16,128]{2,1,0:T(8,128)(2,1)S(1)} collective-permute-done((bf16[8,16,128]{2,1,0:T(8,128)(2,1)S(1)}, bf16[8,16,128]{2,1,0:T(8,128)(2,1)S(1)}, u32[]{:S(2)}, u32[]{:S(2)}) %collective-permute-start.4) | collective-permute-done | bytes 32800 | tf_op jit(solution)/shard_map/ppermute | solution.py:752
  100.9 4.6 %all-to-all-done.3.mine = bf16[32,80,128]{2,1,0:T(8,128)(2,1)S(1)} async-done(((bf16[32,80,128]{2,1,0:T(8,128)(2,1)}), bf16[32,80,128]{2,1,0:T(8,128)(2,1)S(1)}, u32[]{:S(2)}, u32[]{:S(2)}) %all-to-all-start.3) | async-done | bytes 655392 | tf_op jit(solution)/shard_map/all_to_all | solution.py:751
  105.5 6.6 %collective-permute-start.5 = (bf16[32,80,128]{2,1,0:T(8,128)(2,1)S(1)}, bf16[32,80,128]{2,1,0:T(8,128)(2,1)S(1)}, u32[]{:S(2)}, u32[]{:S(2)}) collective-permute-start(bf16[32,80,128]{2,1,0:T(8,128)(2,1)S(1)} %all-to-all-done.3.mine), channel_id=1, source_target_pairs={{0,1},{1,0},{2,3},{3,2},{4,5},{5,4},{6,7},{7,6},{8,9},{9,8},{10,11... | collective-permute-start | bytes 1966088 | tf_op jit(solution)/shard_map/ppermute | solution.py:754
  112.1 1.7 %collective-permute-done.5.other = bf16[32,80,128]{2,1,0:T(8,128)(2,1)S(1)} collective-permute-done((bf16[32,80,128]{2,1,0:T(8,128)(2,1)S(1)}, bf16[32,80,128]{2,1,0:T(8,128)(2,1)S(1)}, u32[]{:S(2)}, u32[]{:S(2)}) %collective-permute-start.5) | collective-permute-done | bytes 655392 | tf_op jit(solution)/shard_map/ppermute | solution.py:754
  113.8 1.6 %shard_map.196 = (bf16[256,1024]{1,0:T(8,128)(2,1)}, bf16[1024,256]{1,0:T(8,128)(2,1)}, bf16[128,256]{1,0:T(8,128)(2,1)}, bf16[9,256]{1,0:T(8,128)(2,1)}, bf16[2...) custom-call(s32[2]{0:T(128)S(1)} %pad_add_fusion.place, bf16[32,80,128]{2,1,0:T(8,128)(2,1)S(1)} %all-to-all-done.3.mine, ...), custom_call_target="tpu_custom_call" | custom-call | bytes 2000000 | tf_op jit(solution)/shard_map/pallas_call | solution.py:49
  (5 shorter events, 1.1 us)
Async XLA Ops:
  2.9 29.9 %all-to-all-start = ((bf16[32,8,128]{2,1,0:T(8,128)(2,1)}), bf16[32,8,128]{2,1,0:T(8,128)(2,1)S(1)}, u32[]{:S(2)}, u32[]{:S(2)}) async-start(bf16[32,8,128]{2,1,0:T(8,128)(2,1)} %get-tuple-element.49), calls=%async_computation | async-start | bytes 131072 | tf_op jit(solution)/shard_map/all_to_all | solution.py:637
  19.7 6.1 %collective-permute-start = (bf16[400,256]{1,0:T(8,128)(2,1)}, bf16[400,256]{1,0:T(8,128)(2,1)S(1)}, u32[]{:S(2)}, u32[]{:S(2)}) collective-permute-start(bf16[400,256]{1,0:T(8,128)(2,1)} %get-tuple-element.52), channel_id=1, source_target_pairs={{0,1},{1,2},{2,3},{3,4},{4,5},{5,6},{6,7},{7,8},{8,9},{9,10},{10,1... | collective-permute-start | bytes 614408 | tf_op jit(solution)/shard_map/ppermute | solution.py:635
  21.3 6.4 %collective-permute-start.1 = (bf16[400,256]{1,0:T(8,128)(2,1)}, bf16[400,256]{1,0:T(8,128)(2,1)S(1)}, u32[]{:S(2)}, u32[]{:S(2)}) collective-permute-start(bf16[400,256]{1,0:T(8,128)(2,1)} %get-tuple-element.53), channel_id=1, source_target_pairs={{1,0},{2,1},{3,2},{4,3},{5,4},{6,5},{7,6},{8,7},{9,8},{10,9},{11,1... | collective-permute-start | bytes 614408 | tf_op jit(solution)/shard_map/ppermute | solution.py:636
  40.2 8.8 %collective-permute-start.2 = (bf16[32,64,128]{2,1,0:T(8,128)(2,1)S(1)}, bf16[32,64,128]{2,1,0:T(8,128)(2,1)S(1)}, u32[]{:S(2)}, u32[]{:S(2)}) collective-permute-start(bf16[32,64,128]{2,1,0:T(8,128)(2,1)S(1)} %get-tuple-element.60), channel_id=1, source_target_pairs={{0,1},{1,0},{2,3},{3,2},{4,5},{5,4},{6,7},{7,6},{8,9},{9,8},{10,11... | collective-permute-start | bytes 1572872 | tf_op jit(solution)/shard_map/ppermute | solution.py:719
  49.9 20.2 %all-to-all-start.1 = ((bf16[32,80,128]{2,1,0:T(8,128)(2,1)}), bf16[32,80,128]{2,1,0:T(8,128)(2,1)S(1)}, u32[]{:S(2)}, u32[]{:S(2)}) async-start(bf16[32,80,128]{2,1,0:T(8,128)(2,1)} %shard_map.192), calls=%async_computation.1 | async-start | bytes 1310720 | tf_op jit(solution)/shard_map/all_to_all | solution.py:722
  59.8 3.1 %collective-permute-start.3 = (bf16[2,2,8,128]{3,2,1,0:T(8,128)(2,1)S(1)}, bf16[2,2,8,128]{3,2,1,0:T(8,128)(2,1)S(1)}, u32[]{:S(2)}, u32[]{:S(2)}) collective-permute-start(bf16[2,2,8,128]{3,2,1,0:T(8,128)(2,1)S(1)} %get-tuple-element.78), channel_id=1, source_target_pairs={{0,1},{1,0},{2,3},{3,2},{4,5},{5,4},{6,7},{7,6},{8,9},{9,8},{10,11... | collective-permute-start | bytes 24584 | tf_op jit(solution)/shard_map/ppermute | solution.py:742
  90.5 15.0 %all-to-all-start.3 = ((bf16[32,80,128]{2,1,0:T(8,128)(2,1)}), bf16[32,80,128]{2,1,0:T(8,128)(2,1)S(1)}, u32[]{:S(2)}, u32[]{:S(2)}) async-start(bf16[32,80,128]{2,1,0:T(8,128)(2,1)} %get-tuple-element.79), calls=%async_computation.3 | async-start | bytes 1310720 | tf_op jit(solution)/shard_map/all_to_all | solution.py:751
  94.8 6.1 %collective-permute-start.4 = (bf16[8,16,128]{2,1,0:T(8,128)(2,1)S(1)}, bf16[8,16,128]{2,1,0:T(8,128)(2,1)S(1)}, u32[]{:S(2)}, u32[]{:S(2)}) collective-permute-start(bf16[8,16,128]{2,1,0:T(8,128)(2,1)S(1)} %get-tuple-element.80.kept), channel_id=1, source_target_pairs={{0,2},{2,0},{1,3},{3,1},{4,6},{6,4},{5,7},{7,5},{8,10},{10,8},{9,1... | collective-permute-start | bytes 98312 | tf_op jit(solution)/shard_map/ppermute | solution.py:752
  105.5 8.3 %collective-permute-start.5 = (bf16[32,80,128]{2,1,0:T(8,128)(2,1)S(1)}, bf16[32,80,128]{2,1,0:T(8,128)(2,1)S(1)}, u32[]{:S(2)}, u32[]{:S(2)}) collective-permute-start(bf16[32,80,128]{2,1,0:T(8,128)(2,1)S(1)} %all-to-all-done.3.mine), channel_id=1, source_target_pairs={{0,1},{1,0},{2,3},{3,2},{4,5},{5,4},{6,7},{7,6},{8,9},{9,8},{10,11... | collective-permute-start | bytes 1966088 | tf_op jit(solution)/shard_map/ppermute | solution.py:754

commit v3 on v2

--- a/solution.py
+++ b/solution.py
@@ -34,7 +34,7 @@
 GELU_B = GELU_A * 0.044715
 
 
-def call(kernel, out_shape, scratch=(), limit=16, flops=0, moved=0, smem=(), far=()):
+def call(kernel, out_shape, scratch=(), limit=16, flops=0, moved=0, smem=(), far=(), out_far=()):
     def run(*args):
         args = [
             pltpu.with_memory_space_constraint(arg, pltpu.HBM) if i in far else arg
@@ -50,7 +50,12 @@
             kernel,
             out_shape=out_shape,
             in_specs=[pl.BlockSpec(memory_space=space(i)) for i in range(len(args))],
-            out_specs=jax.tree.map(lambda _: pl.BlockSpec(memory_space=pltpu.VMEM), out_shape),
+            out_specs=tuple(
+                pl.BlockSpec(memory_space=pltpu.HBM if i in out_far else pltpu.VMEM)
+                for i in range(len(out_shape))
+            )
+            if isinstance(out_shape, tuple)
+            else pl.BlockSpec(memory_space=pltpu.VMEM),
             scratch_shapes=list(scratch),
             compiler_params=pltpu.CompilerParams(vmem_limit_bytes=limit * 2**20),
             cost_estimate=pl.CostEstimate(flops=flops, bytes_accessed=moved, transcendentals=0),
@@ -283,10 +288,11 @@
     xhat,
     rstd,
     hidden,
+    states,
     pre_cot,
     widen,
+    sems,
     shrink,
-    sems,
     normed,
     pres,
     cotangents,
@@ -317,6 +323,8 @@
             state = right[pl.ds((e - 2 - OWN) * ROWS, ROWS), :]
         value = state.astype(F32) + pushed[e * ROWS : (e + 1) * ROWS]
         value = value.astype(BF16).astype(F32)
+        if 2 <= e < 2 + OWN:
+            states[pl.ds((e - 2) * ROWS, ROWS), :] = value.astype(BF16)
         for h in range(2):
             mixed[2 * e + h, pl.ds(8, ROWS), :] = value[:, h * LINK : (h + 1) * LINK]
     tap = taps[...]
@@ -398,11 +406,7 @@
     taps,
     gain,
     widen,
-    hidden,
-    shrink,
-    sea,
     adj_out,
-    succ_out,
     small,
     curve,
     back,
@@ -471,36 +475,44 @@
         if g < 20:
             tail = jnp.concatenate([rest[g // 2 : g // 2 + 1, lanes], tail[1:]], axis=0)
         small[g] = jnp.concatenate([force_grad[g // 2 * 8 : g // 2 * 8 + 8, lanes], tail], axis=0)
-    mlp = dot(hidden[...], shrink[...])
-    for c in range(OWN):
-        mask = sea[pl.ds(c * ROWS, ROWS), :].astype(F32)
-        for h in range(2):
-            lanes = slice(h * LINK, (h + 1) * LINK)
-            state = mixed[2 * (c + 2) + h, pl.ds(8, ROWS), :] + mlp[c * ROWS : (c + 1) * ROWS, lanes]
-            succ_out[pl.ds(c * ROWS, ROWS), lanes] = (mask * state).astype(BF16)
 
 
 def state_kernel(
-    succ,
+    hidden_far,
+    states_far,
+    shrink_far,
+    thermal_far,
+    sea,
     inverse,
     adj,
     place,
-    thermal_far,
     succ_out,
     sst_near,
     sst_across,
     adj_out,
+    hidden,
+    states,
+    shrink,
     thermal,
-    sem,
+    sems,
     turned,
     sums,
 ):
-    wait_for = pltpu.make_async_copy(thermal_far, thermal, sem)
-    wait_for.start()
-    wait_for.wait()
+    copies = fetch(
+        (shrink_far, hidden_far, states_far, thermal_far), (shrink, hidden, states, thermal), sems
+    )
+    for c in range(OWN):
+        put_column(turned, c, adj[pl.ds(c * ROWS, ROWS), :].astype(F32))
+    adj_out[...] = rows_of(turned)
+    for copy in copies:
+        copy.wait()
+    mlp = dot(hidden[...], shrink[...])
     fine = [None, None]
     for c in range(OWN):
-        value = succ[pl.ds(c * ROWS, ROWS), :]
+        rows = slice(c * ROWS, (c + 1) * ROWS)
+        mask = sea[rows, :].astype(F32)
+        mask = jnp.concatenate([mask, mask], axis=1)
+        value = (mask * (states[rows, :].astype(F32) + mlp[rows])).astype(BF16)
         put_column(turned, c, value.astype(F32))
         part = dot(value, thermal[...])
         fine[c // 4] = part if c % 4 == 0 else fine[c // 4] + part
@@ -513,9 +525,6 @@
                 spot = 2 * jnp.bitwise_xor(place[1], other) + core
                 coarse = sum(sums[pl.ds(4 * spot + i, FARS, stride=16), :] for i in range(4))
                 out[other, half] = (coarse * inverse[4 * half + spot]).astype(BF16)
-    for c in range(OWN):
-        put_column(turned, c, adj[pl.ds(c * ROWS, ROWS), :].astype(F32))
-    adj_out[...] = rows_of(turned)
 
 
 def core_sum_kernel(keep, got, small, out):
@@ -662,7 +671,7 @@
         moved=4_000_000,
         far=range(8),
     )(lat[0], adj[0], drive, taps, gain_row, water_t, sites_t, margin_t)
-    keep, send, mixed, forcing, xhat, rstd, hidden, pre_cot, widen, shrink = call(
+    keep, send, mixed, forcing, xhat, rstd, hidden, states, pre_cot, widen = call(
         ocean_kernel,
         (
             held(CHUNKS, BIG, LINK, dtype=F32),
@@ -672,12 +681,13 @@
             held(MID * ROWS, CH, dtype=F32),
             held(MID * ROWS, LINK, dtype=F32),
             held(CELLS, HID),
+            held(CELLS, CH),
             held(MID * ROWS, HID),
             held(CH, HID),
-            held(HID, CH),
         ),
         [
             pltpu.SemaphoreType.DMA((2,)),
+            pltpu.VMEM((HID, CH), BF16),
             pltpu.VMEM((MID * ROWS, CH), BF16),
             pltpu.VMEM((2, MID * ROWS, CH), F32),
             pltpu.VMEM((2, MID * ROWS, CH), F32),
@@ -704,21 +714,21 @@
         widen,
         shrink,
     )
-    adj_turned, succ_turned, small = call(
+    adj_turned, small = call(
         rest_kernel,
-        (held(CELLS, CH), held(CELLS, CH), held(CHUNKS, 16, LINK, dtype=F32)),
+        (held(CELLS, CH), held(CHUNKS, 16, LINK, dtype=F32)),
         [
             pltpu.VMEM((2 * MID, PAD, LINK), F32),
             pltpu.VMEM((MID * ROWS, CH), F32),
         ],
         flops=1_000_000_000,
         moved=8_000_000,
-    )(mixed, forcing, xhat, rstd, pre_cot, cot, taps, gain_row, widen, hidden, shrink, sea)
+    )(mixed, forcing, xhat, rstd, pre_cot, cot, taps, gain_row, widen)
 
     swap = [(0, 1), (1, 0)]
     got = lax.ppermute(send, "core", swap)
     stage = call(core_sum_kernel, held(CHUNKS, CHUNK, LINK), moved=2_000_000)(keep, got, small)
-    stage, succ_turned = lax.optimization_barrier((stage, succ_turned))
+    stage, hidden, adj_turned = lax.optimization_barrier((stage, hidden, adj_turned))
     stage = lax.all_to_all(stage, GROUP, 0, 0, tiled=True)
     succ, sst_near, sst_across, adj_out = call(
         state_kernel,
@@ -729,16 +739,19 @@
             shape(ROWS, OWN, CH),
         ),
         [
+            pltpu.VMEM((CELLS, HID), BF16),
+            pltpu.VMEM((CELLS, CH), BF16),
+            pltpu.VMEM((HID, CH), BF16),
             pltpu.VMEM((CH, LINK), BF16),
-            pltpu.SemaphoreType.DMA(()),
+            pltpu.SemaphoreType.DMA((4,)),
             pltpu.VMEM((2 * CELLS, LINK), F32),
             pltpu.VMEM((ROWS, LINK), F32),
         ],
         flops=1_000_000_000,
         moved=5_000_000,
-        smem=(3,),
-        far=(4,),
-    )(succ_turned, inverse, adj_turned, place, thermal)
+        smem=(7,),
+        far=range(4),
+    )(hidden, states, shrink, thermal, sea, inverse, adj_turned, place)
     across = lax.ppermute(sst_across, "core", swap)
     stage = call(group_sum_kernel, held(FARS, PIECE, LINK), moved=700_000)(stage, sst_near, across)
     stage = lax.all_to_all(stage, "far", 0, 0, tiled=True)

time: 116 us -> 115 us (level)
  waiting for transfers between devices: 26.6 us -> 25.1 us
    all_to_all x2, waiting for transfers between devices: 11.8 us -> 10.3 us  [body(): stage = lax.all_to_all(stage, GROUP, 0, 0, tiled=True)]
where the time goes in v3:
time: 115 us; the launch traced here: 114 us
  starting transfers between devices  45.5 us (40%)
  waiting for transfers between devices  25.1 us (22%)
  Pallas kernels  23.5 us (20%)
  blocking collectives  19.3 us (17%)
    pallas_call x9, Pallas kernels, run(): pl.pallas_call(kernel, out_shape=out_shape, in_specs=[pl.BlockSpec(memory...  23.5 us
    all_to_all x1, blocking collectives, body(): stage = lax.all_to_all(stage, 'far', 0, 0, tiled=True)  19.3 us
    all_to_all x1, starting transfers between devices, body(): flux_in = lax.all_to_all(fluxes, TILE, 0, 0, tiled=True)  16.8 us
    all_to_all x2, starting transfers between devices, body(): stage = lax.all_to_all(stage, GROUP, 0, 0, tiled=True)  11.4 us
    all_to_all x2, waiting for transfers between devices, body(): stage = lax.all_to_all(stage, GROUP, 0, 0, tiled=True)  10.3 us
    ppermute x1, starting transfers between devices, body(): other = lax.ppermute(stage, 'core', swap)  6.6 us
    all_to_all x1, waiting for transfers between devices, body(): flux_in = lax.all_to_all(fluxes, TILE, 0, 0, tiled=True)  5.02 us
    ppermute x1, starting transfers between devices, body(): got = lax.ppermute(send, 'core', swap)  3.77 us
  transfers between devices with their start and end apart: 9, of which 8 were waited for; matrix products, arithmetic and copies ran while one was open for 0% of the time, Pallas kernels for 9%

profile of v3, /device:TPU:1, one launch (start us, length us, event | category | flops | bytes accessed | tf_op | source)
XLA Modules:
  0.0 114.2 jit_solution(17017318287643168917)
XLA Ops:
  0.6 2.3 %shard_map.188 = (bf16[32,8,128]{2,1,0:T(8,128)(2,1)}, bf16[400,256]{1,0:T(8,128)(2,1)}, bf16[400,256]{1,0:T(8,128)(2,1)}) custom-call(bf16[64,384]{1,0:T(8,128)(2,1)} %bitcast.22, bf16[384,128]{1,0:T(8,128)(2,1)} %head_far.1, bf16[128,8,256]{2,1,0:T(8,128)(2,1)} %bitcast.14, bf16[128,8,256]{2,1,0:T(8,128)(2,1)} %bitcast.16, s32[8,128]{1,0:T(8,128)} %bitcast.23, ...), custom_call_target="tpu_custom_call" | custom-call | bytes 2000000 | tf_op jit(solution)/shard_map/pallas_call | solution.py:49
  2.9 16.8 %all-to-all-start = ((bf16[32,8,128]{2,1,0:T(8,128)(2,1)}), bf16[32,8,128]{2,1,0:T(8,128)(2,1)S(1)}, u32[]{:S(2)}, u32[]{:S(2)}) async-start(bf16[32,8,128]{2,1,0:T(8,128)(2,1)} %get-tuple-element.49), calls=%async_computation | async-start | bytes 131072 | tf_op jit(solution)/shard_map/all_to_all | solution.py:646
  19.7 1.6 %collective-permute-start = (bf16[400,256]{1,0:T(8,128)(2,1)}, bf16[400,256]{1,0:T(8,128)(2,1)S(1)}, u32[]{:S(2)}, u32[]{:S(2)}) collective-permute-start(bf16[400,256]{1,0:T(8,128)(2,1)} %get-tuple-element.52), channel_id=1, source_target_pairs={{0,1},{1,2},{2,3},{3,4},{4,5},{5,6},{6,7},{7,8},{8,9},{9,10},{10,1... | collective-permute-start | bytes 614408 | tf_op jit(solution)/shard_map/ppermute | solution.py:644
  21.4 2.1 %shard_map.189 = (bf16[1024,256]{1,0:T(8,128)(2,1)S(1)}, bf16[1024,256]{1,0:T(8,128)(2,1)S(1)}, bf16[256,1024]{1,0:T(8,128)(2,1)S(1)}, bf16[1024,128]{1,0:T(8,12...) custom-call(bf16[128,8,256]{2,1,0:T(8,128)(2,1)} %bitcast.15, ...), custom_call_target="tpu_custom_call" | custom-call | bytes 4000000 | tf_op jit(solution)/shard_map/pallas_call | solution.py:49
  23.6 2.3 %collective-permute-done.left = bf16[400,256]{1,0:T(8,128)(2,1)S(1)} collective-permute-done((bf16[400,256]{1,0:T(8,128)(2,1)}, bf16[400,256]{1,0:T(8,128)(2,1)S(1)}, u32[]{:S(2)}, u32[]{:S(2)}) %collective-permute-start) | collective-permute-done | bytes 204832 | tf_op jit(solution)/shard_map/ppermute | solution.py:644
  25.8 1.9 %collective-permute-done.1.right = bf16[400,256]{1,0:T(8,128)(2,1)S(1)} collective-permute-done((bf16[400,256]{1,0:T(8,128)(2,1)}, bf16[400,256]{1,0:T(8,128)(2,1)S(1)}, u32[]{:S(2)}, u32[]{:S(2)}) %collective-permute-start.1) | collective-permute-done | bytes 204832 | tf_op jit(solution)/shard_map/ppermute | solution.py:645
  27.8 5.0 %all-to-all-done = bf16[32,8,128]{2,1,0:T(8,128)(2,1)S(1)} async-done(((bf16[32,8,128]{2,1,0:T(8,128)(2,1)}), bf16[32,8,128]{2,1,0:T(8,128)(2,1)S(1)}, u32[]{:S(2)}, u32[]{:S(2)}) %all-to-all-start) | async-done | bytes 65568 | tf_op jit(solution)/shard_map/all_to_all | solution.py:646
  32.8 7.8 %shard_map.190 = (f32[32,64,128]{2,1,0:T(8,128)S(1)}, bf16[32,64,128]{2,1,0:T(8,128)(2,1)S(1)}, f32[24,144,128]{2,1,0:T(8,128)S(1)}, bf16[1024,128]{1,0:T(8,128)...) custom-call(s32[2]{0:T(128)S(1)} %pad_add_fusion.place, ...), custom_call_target="tpu_custom_call" | custom-call | flops 4000000000 | bytes 10000000 | tf_op jit(solution)/shard_map/pallas_call | solution.py:49
  40.6 3.8 %collective-permute-start.2 = (bf16[32,64,128]{2,1,0:T(8,128)(2,1)S(1)}, bf16[32,64,128]{2,1,0:T(8,128)(2,1)S(1)}, u32[]{:S(2)}, u32[]{:S(2)}) collective-permute-start(bf16[32,64,128]{2,1,0:T(8,128)(2,1)S(1)} %get-tuple-element.60), channel_id=1, source_target_pairs={{0,1},{1,0},{2,3},{3,2},{4,5},{5,4},{6,7},{7,6},{8,9},{9,8},{10,11... | collective-permute-start | bytes 1572872 | tf_op jit(solution)/shard_map/ppermute | solution.py:729
  44.4 3.3 %shard_map.191 = (bf16[1024,256]{1,0:T(8,128)(2,1)S(1)}, f32[32,16,128]{2,1,0:T(8,128)S(1)}) custom-call(f32[24,144,128]{2,1,0:T(8,128)S(1)} %get-tuple-element.61.mixed, bf16[1024,128]{1,0:T(8,128)(2,1)S(1)} %get-tuple-element.62.forcing, f32[1280,256]{1,0:T(8,128)S(1)} %get-tuple-element.63.xhat, f32[1280,128]{1,0:T(8,128)S(1)} %get-tuple-element.64.rstd, ...), custom_call_target="tpu_custom_call" | custom-call | flops 1000000000 | bytes 8000000 | tf_op jit(solution)/shard_map/pallas_call | solution.py:49
  47.7 1.0 shard_map.192
  48.7 7.0 %all-to-all-start.1 = ((bf16[32,80,128]{2,1,0:T(8,128)(2,1)}), bf16[32,80,128]{2,1,0:T(8,128)(2,1)S(1)}, u32[]{:S(2)}, u32[]{:S(2)}) async-start(bf16[32,80,128]{2,1,0:T(8,128)(2,1)} %shard_map.192), calls=%async_computation.1 | async-start | bytes 1310720 | tf_op jit(solution)/shard_map/all_to_all | solution.py:732
  55.7 4.4 %shard_map.193 = (bf16[128,8,256]{2,1,0:T(8,128)(2,1)}, bf16[2,2,8,128]{3,2,1,0:T(8,128)(2,1)S(1)}, bf16[2,2,8,128]{3,2,1,0:T(8,128)(2,1)S(1)}, bf16[128,8,256]{2,1,0:T(8,128)(2,1)}) custom-call(bf16[1024,1024]{1,0:T(8,128)(2,1)} %copy-done, bf16[1024,256]{1,0:T(8,128)(2,1)} %copy-done.1, bf16[1024,256]{1,0:T(8,128)(2,1)} %shrink_far.3, ...), custom_call_target="tpu_custom_call" | custom-call | flops 1000000000 | bytes 5000000 | tf_op jit(solution)/shard_map/pallas_call | solution.py:49
  60.1 2.2 %collective-permute-start.3 = (bf16[2,2,8,128]{3,2,1,0:T(8,128)(2,1)S(1)}, bf16[2,2,8,128]{3,2,1,0:T(8,128)(2,1)S(1)}, u32[]{:S(2)}, u32[]{:S(2)}) collective-permute-start(bf16[2,2,8,128]{3,2,1,0:T(8,128)(2,1)S(1)} %get-tuple-element.78), channel_id=1, source_target_pairs={{0,1},{1,0},{2,3},{3,2},{4,5},{5,4},{6,7},{7,6},{8,9},{9,8},{10,11... | collective-permute-start | bytes 24584 | tf_op jit(solution)/shard_map/ppermute | solution.py:755
  63.2 5.7 %all-to-all-done.1.got = bf16[32,80,128]{2,1,0:T(8,128)(2,1)S(1)} async-done(((bf16[32,80,128]{2,1,0:T(8,128)(2,1)}), bf16[32,80,128]{2,1,0:T(8,128)(2,1)S(1)}, u32[]{:S(2)}, u32[]{:S(2)}) %all-to-all-start.1) | async-done | bytes 655392 | tf_op jit(solution)/shard_map/all_to_all | solution.py:732
  69.0 19.3 %all_to_all.20.got = bf16[8,96,128]{2,1,0:T(8,128)(2,1)S(1)} all-to-all(bf16[8,96,128]{2,1,0:T(8,128)(2,1)S(1)} %shard_map.194), channel_id=1, replica_groups=mesh['ens_0'=4,'ens_1'=4,'far'=8,'near'=2,'core'=2] {'far'}, dimensions={0} | all-to-all | bytes 393216 | tf_op jit(solution)/shard_map/all_to_all | solution.py:757
  88.3 0.9 shard_map.195
  89.2 4.3 %all-to-all-start.3 = ((bf16[32,80,128]{2,1,0:T(8,128)(2,1)}), bf16[32,80,128]{2,1,0:T(8,128)(2,1)S(1)}, u32[]{:S(2)}, u32[]{:S(2)}) async-start(bf16[32,80,128]{2,1,0:T(8,128)(2,1)} %get-tuple-element.79), calls=%async_computation.3 | async-start | bytes 1310720 | tf_op jit(solution)/shard_map/all_to_all | solution.py:764
  93.5 3.1 %collective-permute-start.4 = (bf16[8,16,128]{2,1,0:T(8,128)(2,1)S(1)}, bf16[8,16,128]{2,1,0:T(8,128)(2,1)S(1)}, u32[]{:S(2)}, u32[]{:S(2)}) collective-permute-start(bf16[8,16,128]{2,1,0:T(8,128)(2,1)S(1)} %get-tuple-element.80.kept), channel_id=1, source_target_pairs={{0,2},{2,0},{1,3},{3,1},{4,6},{6,4},{5,7},{7,5},{8,10},{10,8},{9,1... | collective-permute-start | bytes 98312 | tf_op jit(solution)/shard_map/ppermute | solution.py:765
  96.7 3.0 %collective-permute-done.4.moved = bf16[8,16,128]{2,1,0:T(8,128)(2,1)S(1)} collective-permute-done((bf16[8,16,128]{2,1,0:T(8,128)(2,1)S(1)}, bf16[8,16,128]{2,1,0:T(8,128)(2,1)S(1)}, u32[]{:S(2)}, u32[]{:S(2)}) %collective-permute-start.4) | collective-permute-done | bytes 32800 | tf_op jit(solution)/shard_map/ppermute | solution.py:765
  99.7 4.6 %all-to-all-done.3.mine = bf16[32,80,128]{2,1,0:T(8,128)(2,1)S(1)} async-done(((bf16[32,80,128]{2,1,0:T(8,128)(2,1)}), bf16[32,80,128]{2,1,0:T(8,128)(2,1)S(1)}, u32[]{:S(2)}, u32[]{:S(2)}) %all-to-all-start.3) | async-done | bytes 655392 | tf_op jit(solution)/shard_map/all_to_all | solution.py:764
  104.2 6.6 %collective-permute-start.5 = (bf16[32,80,128]{2,1,0:T(8,128)(2,1)S(1)}, bf16[32,80,128]{2,1,0:T(8,128)(2,1)S(1)}, u32[]{:S(2)}, u32[]{:S(2)}) collective-permute-start(bf16[32,80,128]{2,1,0:T(8,128)(2,1)S(1)} %all-to-all-done.3.mine), channel_id=1, source_target_pairs={{0,1},{1,0},{2,3},{3,2},{4,5},{5,4},{6,7},{7,6},{8,9},{9,8},{10,11... | collective-permute-start | bytes 1966088 | tf_op jit(solution)/shard_map/ppermute | solution.py:767
  110.8 1.7 %collective-permute-done.5.other = bf16[32,80,128]{2,1,0:T(8,128)(2,1)S(1)} collective-permute-done((bf16[32,80,128]{2,1,0:T(8,128)(2,1)S(1)}, bf16[32,80,128]{2,1,0:T(8,128)(2,1)S(1)}, u32[]{:S(2)}, u32[]{:S(2)}) %collective-permute-start.5) | collective-permute-done | bytes 655392 | tf_op jit(solution)/shard_map/ppermute | solution.py:767
  112.5 1.6 %shard_map.196 = (bf16[256,1024]{1,0:T(8,128)(2,1)}, bf16[1024,256]{1,0:T(8,128)(2,1)}, bf16[128,256]{1,0:T(8,128)(2,1)}, bf16[9,256]{1,0:T(8,128)(2,1)}, bf16[2...) custom-call(s32[2]{0:T(128)S(1)} %pad_add_fusion.place, bf16[32,80,128]{2,1,0:T(8,128)(2,1)S(1)} %all-to-all-done.3.mine, ...), custom_call_target="tpu_custom_call" | custom-call | bytes 2000000 | tf_op jit(solution)/shard_map/pallas_call | solution.py:49
  (9 shorter events, 1.1 us)
Async XLA Ops:
  2.9 29.9 %all-to-all-start = ((bf16[32,8,128]{2,1,0:T(8,128)(2,1)}), bf16[32,8,128]{2,1,0:T(8,128)(2,1)S(1)}, u32[]{:S(2)}, u32[]{:S(2)}) async-start(bf16[32,8,128]{2,1,0:T(8,128)(2,1)} %get-tuple-element.49), calls=%async_computation | async-start | bytes 131072 | tf_op jit(solution)/shard_map/all_to_all | solution.py:646
  19.7 6.1 %collective-permute-start = (bf16[400,256]{1,0:T(8,128)(2,1)}, bf16[400,256]{1,0:T(8,128)(2,1)S(1)}, u32[]{:S(2)}, u32[]{:S(2)}) collective-permute-start(bf16[400,256]{1,0:T(8,128)(2,1)} %get-tuple-element.52), channel_id=1, source_target_pairs={{0,1},{1,2},{2,3},{3,4},{4,5},{5,6},{6,7},{7,8},{8,9},{9,10},{10,1... | collective-permute-start | bytes 614408 | tf_op jit(solution)/shard_map/ppermute | solution.py:644
  21.3 6.4 %collective-permute-start.1 = (bf16[400,256]{1,0:T(8,128)(2,1)}, bf16[400,256]{1,0:T(8,128)(2,1)S(1)}, u32[]{:S(2)}, u32[]{:S(2)}) collective-permute-start(bf16[400,256]{1,0:T(8,128)(2,1)} %get-tuple-element.53), channel_id=1, source_target_pairs={{1,0},{2,1},{3,2},{4,3},{5,4},{6,5},{7,6},{8,7},{9,8},{10,9},{11,1... | collective-permute-start | bytes 614408 | tf_op jit(solution)/shard_map/ppermute | solution.py:645
  40.6 7.1 %copy-start = (bf16[1024,1024]{1,0:T(8,128)(2,1)}, bf16[1024,1024]{1,0:T(8,128)(2,1)S(1)}, u32[]{:S(2)}) copy-start(bf16[1024,1024]{1,0:T(8,128)(2,1)S(1)} %get-tuple-element.70.hidden_far) | copy-start | bytes 6291460
  40.6 7.1 %copy-start.1 = (bf16[1024,256]{1,0:T(8,128)(2,1)}, bf16[1024,256]{1,0:T(8,128)(2,1)S(1)}, u32[]{:S(2)}) copy-start(bf16[1024,256]{1,0:T(8,128)(2,1)S(1)} %get-tuple-element.71.states_far) | copy-start | bytes 1572868
  40.6 7.1 %collective-permute-start.2 = (bf16[32,64,128]{2,1,0:T(8,128)(2,1)S(1)}, bf16[32,64,128]{2,1,0:T(8,128)(2,1)S(1)}, u32[]{:S(2)}, u32[]{:S(2)}) collective-permute-start(bf16[32,64,128]{2,1,0:T(8,128)(2,1)S(1)} %get-tuple-element.60), channel_id=1, source_target_pairs={{0,1},{1,0},{2,3},{3,2},{4,5},{5,4},{6,7},{7,6},{8,9},{9,8},{10,11... | collective-permute-start | bytes 1572872 | tf_op jit(solution)/shard_map/ppermute | solution.py:729
  48.7 20.2 %all-to-all-start.1 = ((bf16[32,80,128]{2,1,0:T(8,128)(2,1)}), bf16[32,80,128]{2,1,0:T(8,128)(2,1)S(1)}, u32[]{:S(2)}, u32[]{:S(2)}) async-start(bf16[32,80,128]{2,1,0:T(8,128)(2,1)} %shard_map.192), calls=%async_computation.1 | async-start | bytes 1310720 | tf_op jit(solution)/shard_map/all_to_all | solution.py:732
  60.1 3.1 %collective-permute-start.3 = (bf16[2,2,8,128]{3,2,1,0:T(8,128)(2,1)S(1)}, bf16[2,2,8,128]{3,2,1,0:T(8,128)(2,1)S(1)}, u32[]{:S(2)}, u32[]{:S(2)}) collective-permute-start(bf16[2,2,8,128]{3,2,1,0:T(8,128)(2,1)S(1)} %get-tuple-element.78), channel_id=1, source_target_pairs={{0,1},{1,0},{2,3},{3,2},{4,5},{5,4},{6,7},{7,6},{8,9},{9,8},{10,11... | collective-permute-start | bytes 24584 | tf_op jit(solution)/shard_map/ppermute | solution.py:755
  89.2 15.0 %all-to-all-start.3 = ((bf16[32,80,128]{2,1,0:T(8,128)(2,1)}), bf16[32,80,128]{2,1,0:T(8,128)(2,1)S(1)}, u32[]{:S(2)}, u32[]{:S(2)}) async-start(bf16[32,80,128]{2,1,0:T(8,128)(2,1)} %get-tuple-element.79), calls=%async_computation.3 | async-start | bytes 1310720 | tf_op jit(solution)/shard_map/all_to_all | solution.py:764
  93.5 6.1 %collective-permute-start.4 = (bf16[8,16,128]{2,1,0:T(8,128)(2,1)S(1)}, bf16[8,16,128]{2,1,0:T(8,128)(2,1)S(1)}, u32[]{:S(2)}, u32[]{:S(2)}) collective-permute-start(bf16[8,16,128]{2,1,0:T(8,128)(2,1)S(1)} %get-tuple-element.80.kept), channel_id=1, source_target_pairs={{0,2},{2,0},{1,3},{3,1},{4,6},{6,4},{5,7},{7,5},{8,10},{10,8},{9,1... | collective-permute-start | bytes 98312 | tf_op jit(solution)/shard_map/ppermute | solution.py:765
  104.2 8.3 %collective-permute-start.5 = (bf16[32,80,128]{2,1,0:T(8,128)(2,1)S(1)}, bf16[32,80,128]{2,1,0:T(8,128)(2,1)S(1)}, u32[]{:S(2)}, u32[]{:S(2)}) collective-permute-start(bf16[32,80,128]{2,1,0:T(8,128)(2,1)S(1)} %all-to-all-done.3.mine), channel_id=1, source_target_pairs={{0,1},{1,0},{2,3},{3,2},{4,5},{5,4},{6,7},{7,6},{8,9},{9,8},{10,11... | collective-permute-start | bytes 1966088 | tf_op jit(solution)/shard_map/ppermute | solution.py:767
